TPU v7x, 32 devices: a whole 2x2x4 slice. The times are simulated.
32 devices in a mesh: groups: 2 (over y), dom: 8 (over z, x), sub: 2 (over core).
Axes of the slice: x: 2, y: 2, z: 4, core: 2. Of those that a mesh axis runs over, the one named last changes fastest.
Arguments:
- features: bfloat16 [524288, 128], P(('groups', 'dom', 'sub')), parts along dimension 0, may hold values from -6 to 6
- fine_nbrs: int32 [6, 524288], P(None, ('groups', 'dom', 'sub')), parts along dimension 1, may hold values from 0 to 17919
- send_rows: int32 [16384], P(('groups', 'dom', 'sub')), parts along dimension 0, may hold values from 0 to 16383
- cluster: int32 [524288], P(('groups', 'dom', 'sub')), parts along dimension 0, may hold values from 0 to 32767, as said below
- coarse_send: int32 [8192], P(('groups', 'dom', 'sub')), parts along dimension 0, may hold values from 0 to 2047
- coarse_nbrs: int32 [6, 65536], P(None, ('groups', 'dom', 'sub')), parts along dimension 1, may hold values from 0 to 2815
- edge_weights: bfloat16 [2, 3, 128, 128], replicated, may hold values from -0.5 to 0.5
- node_weights: bfloat16 [2, 3, 128, 128], replicated, may hold values from -0.5 to 0.5
- biases: float32 [2, 2, 128], replicated, may hold values from -3 to 3
Outputs:
- nodes: bfloat16 [524288, 128], P(('groups', 'dom', 'sub')), parts along dimension 0
- coarse_update: bfloat16 [65536, 128], P(('groups', 'dom', 'sub')), parts along dimension 0
There are 2 independent parts, one for each index of `groups`. A program takes and returns all parts, laid end to end along the dimension named above; an argument that names none is the same for every part. Nothing has to cross between parts.
Inputs may be any that keep to these rules, and one draw needn't show every extreme that they name: `cluster`: every coarse node has exactly 8 fine nodes. Coarse node c belongs to partition c // 2048. Of the fine nodes of partition p, exactly 14848 have their coarse node in partition p, and exactly 512 in partition p + k modulo 16, for each k = 1 .. 3.
All inputs are finite; a program needn't handle non-finite values.
Results may differ from a plain program's by a relative error of at most 0.019.
Values may be sent and summed in bfloat16 or wider, within the bound.
A program may use at most 128 MiB of HBM per device.

v0:
```python
import jax
import jax.numpy as jnp
from jax import lax
from jax.sharding import PartitionSpec as P

RATIO = 8
REACH = 4


def extended(block, sides, width):
    for axis, dim in sides:
        count = lax.axis_size(axis)
        forward = [(i, i + 1) for i in range(count - 1)]
        forward.append((count - 1, 0))
        backward = [(target, source) for source, target in forward]
        low = lax.ppermute(
            lax.slice_in_dim(block, block.shape[dim] - width, None, axis=dim), axis, forward
        )
        high = lax.ppermute(lax.slice_in_dim(block, 0, width, axis=dim), axis, backward)
        block = jnp.concatenate([low, block, high], axis=dim)
    return block


def from_behind(block, axis, distance):
    devices = range(lax.axis_size(axis))
    route = [((i - distance) % len(devices), i) for i in devices]
    return lax.ppermute(block, axis, route)


def message_layer(states, table, neighbor_idx, edge_proj, node_proj, bias_pair):
    count_rows = states.shape[0]
    block_rows = min(2048, count_rows)
    num_blocks = count_rows // block_rows
    far_term = jnp.dot(table, edge_proj[1], preferred_element_type=jnp.float32)

    def one_block(block_index):
        row_block = lax.dynamic_slice_in_dim(states, block_index * block_rows, block_rows, 0)
        nbr_block = lax.dynamic_slice_in_dim(neighbor_idx, block_index * block_rows, block_rows, 1)
        own_term = jnp.dot(row_block, edge_proj[0], preferred_element_type=jnp.float32)
        pre_act = own_term[None] + far_term[nbr_block] + bias_pair[0]
        hidden = jax.nn.silu(pre_act).astype(jnp.bfloat16)
        messages = jax.nn.silu(
            jnp.einsum("kbh,hg->kbg", hidden, edge_proj[2], preferred_element_type=jnp.float32)
        )
        gathered_msgs = jnp.sum(messages, axis=0).astype(jnp.bfloat16)
        inner = jax.nn.silu(
            jnp.dot(row_block, node_proj[0], preferred_element_type=jnp.float32)
            + jnp.dot(gathered_msgs, node_proj[1], preferred_element_type=jnp.float32)
            + bias_pair[1]
        ).astype(jnp.bfloat16)
        return jnp.dot(inner, node_proj[2], preferred_element_type=jnp.float32)

    result = lax.map(one_block, jnp.arange(num_blocks, dtype=jnp.int32))
    return result.reshape(count_rows, -1)


def on_device(
    features,
    fine_nbrs,
    send_rows,
    cluster,
    coarse_send,
    coarse_nbrs,
    edge_weights,
    node_weights,
    biases,
):
    local_rows = features.shape[0]
    width = features.shape[1]
    coarse_rows = local_rows // RATIO
    spill = local_rows // 32
    local_count = local_rows - (REACH - 1) * spill
    outgoing = features[send_rows]
    halo_rows = extended(outgoing, ((("dom", "sub"), 0),), outgoing.shape[0])
    neighbor_table = jnp.concatenate([features, halo_rows], axis=0)
    update = message_layer(
        features, neighbor_table, fine_nbrs, edge_weights[0], node_weights[0], biases[0]
    )
    fine_out = (features.astype(jnp.float32) + update).astype(jnp.bfloat16)
    num_parts = lax.axis_size(("dom", "sub"))
    position = lax.axis_index(("dom", "sub"))
    owner_part = cluster // coarse_rows
    reach_index = (owner_part - position) % num_parts
    slot_index = cluster % coarse_rows
    combined_key = reach_index * coarse_rows + slot_index
    ordering = jnp.argsort(combined_key, stable=True)
    remote = ordering[local_count:].reshape(REACH - 1, spill)
    leaving_rows = fine_out[remote]
    leaving_slots = slot_index[remote]
    arrived_rows = []
    arrived_slots = []
    for distance in range(1, REACH):
        got_rows, got_slots = from_behind(
            (leaving_rows[distance - 1], leaving_slots[distance - 1]), ("dom", "sub"), distance
        )
        arrived_rows.append(got_rows)
        arrived_slots.append(got_slots)
    member_rows = jnp.concatenate([fine_out] + arrived_rows, axis=0)
    member_keys = jnp.concatenate(
        [jnp.where(reach_index == 0, slot_index, coarse_rows)] + arrived_slots, axis=0
    )
    grouped = jnp.argsort(member_keys.astype(jnp.int32), stable=True)[: coarse_rows * RATIO]
    cluster_sum = jnp.sum(
        member_rows[grouped].reshape(coarse_rows, RATIO, width).astype(jnp.float32), axis=1
    )
    coarse_in = (cluster_sum * (1.0 / RATIO)).astype(jnp.bfloat16)
    coarse_out = coarse_in[coarse_send]
    coarse_halo = extended(coarse_out, ((("dom", "sub"), 0),), coarse_out.shape[0])
    coarse_table = jnp.concatenate([coarse_in, coarse_halo], axis=0)
    coarse_update = message_layer(
        coarse_in, coarse_table, coarse_nbrs, edge_weights[1], node_weights[1], biases[1]
    ).astype(jnp.bfloat16)
    returned = []
    for distance in range(1, REACH):
        returned.append(from_behind(coarse_update, ("dom", "sub"), -distance))
    lookup = jnp.concatenate([coarse_update] + returned, axis=0)
    nodes = (fine_out.astype(jnp.float32) + lookup[combined_key].astype(jnp.float32)).astype(
        jnp.bfloat16
    )
    return (nodes, coarse_update)


def solution(mesh):
    return jax.shard_map(
        on_device,
        mesh=mesh,
        in_specs=(
            P(("groups", "dom", "sub"), None),
            P(None, ("groups", "dom", "sub")),
            P(("groups", "dom", "sub")),
            P(("groups", "dom", "sub")),
            P(("groups", "dom", "sub")),
            P(None, ("groups", "dom", "sub")),
            P(),
            P(),
            P(),
        ),
        out_specs=(P(("groups", "dom", "sub"), None), P(("groups", "dom", "sub"), None)),
        check_vma=False,
    )
```

profile of v0, /device:TPU:0, one launch (start us, length us, event | category | flops | bytes accessed | tf_op | source)
XLA Modules:
  0.0 791.6 jit_solution(8391380211355136251)
XLA Ops:
  12.3 7.7 sort.34
  20.1 8.4 %gather_fusion.3 = s32[1536]{0:T(1024)S(1)} fusion(s32[16384]{0:T(1024)S(1)} %get-tuple-element.104, s32[2048]{0:T(1024)S(1)} %pad_clamp_fusion), kind=kCustom, calls=%fused_computation.3 | custom fusion | bytes 18432 | tf_op jit(solution)/shard_map/gather | solution.py:89
  35.0 11.3 %sort.35 = (s32[17920]{0:T(1024)}, s32[17920]{0:T(1024)}) sort(s32[17920]{0:T(1024)S(1)} %pad_add_fusion, s32[17920]{0:T(1024)S(1)} %iota.13), dimensions={0}, to_apply=%region_4.5 | sort | flops 268800 | bytes 286720 | tf_op jit(solution)/shard_map/jit(argsort)/sort | solution.py:102
  46.3 7.1 fusion.28
  53.3 460.3 %while.2 = (s32[]{:T(128)}, f32[8,2048,128]{2,1,0:T(8,128)}, s32[8]{0:T(128)S(1)}, bf16[16384,128]{1,0:T(8,128)(2,1)}, bf16[3,128,128]{2,1,0:T(8,128)(2,1)S(1)},...) while((s32[]{:T(128)}, f32[8,2048,128]{2,1,0:T(8,128)}, ...), condition=%wide.region_2.3_spmd, body=%wide.region_0.2_spmd.sunk | while | flops 691585024 | bytes 26726084 | solution.py:53
  57.2 45.0 %gather_fusion = f32[12288,128]{1,0:T(8,128)} fusion(f32[17920,128]{1,0:T(8,128)} %get-tuple-element.206, s32[12288]{0:T(1024)S(1)} %broadcast_clamp_fusion.3), kind=kCustom, calls=%fused_computation.clone.1 | custom fusion | bytes 12632064 | tf_op jit(solution)/shard_map/while/body/eval_jaxpr/gather | solution.py:40
  102.2 6.2 multiply_reduce_fusion.3
  114.7 45.0 %gather_fusion = f32[12288,128]{1,0:T(8,128)} fusion(f32[17920,128]{1,0:T(8,128)} %get-tuple-element.206, s32[12288]{0:T(1024)S(1)} %broadcast_clamp_fusion.3), kind=kCustom, calls=%fused_computation.clone.1 | custom fusion | bytes 12632064 | tf_op jit(solution)/shard_map/while/body/eval_jaxpr/gather | solution.py:40
  159.6 6.2 multiply_reduce_fusion.3
  172.1 45.0 %gather_fusion = f32[12288,128]{1,0:T(8,128)} fusion(f32[17920,128]{1,0:T(8,128)} %get-tuple-element.206, s32[12288]{0:T(1024)S(1)} %broadcast_clamp_fusion.3), kind=kCustom, calls=%fused_computation.clone.1 | custom fusion | bytes 12632064 | tf_op jit(solution)/shard_map/while/body/eval_jaxpr/gather | solution.py:40
  217.1 6.2 multiply_reduce_fusion.3
  229.6 45.0 %gather_fusion = f32[12288,128]{1,0:T(8,128)} fusion(f32[17920,128]{1,0:T(8,128)} %get-tuple-element.206, s32[12288]{0:T(1024)S(1)} %broadcast_clamp_fusion.3), kind=kCustom, calls=%fused_computation.clone.1 | custom fusion | bytes 12632064 | tf_op jit(solution)/shard_map/while/body/eval_jaxpr/gather | solution.py:40
  274.6 6.2 multiply_reduce_fusion.3
  287.2 45.0 %gather_fusion = f32[12288,128]{1,0:T(8,128)} fusion(f32[17920,128]{1,0:T(8,128)} %get-tuple-element.206, s32[12288]{0:T(1024)S(1)} %broadcast_clamp_fusion.3), kind=kCustom, calls=%fused_computation.clone.1 | custom fusion | bytes 12632064 | tf_op jit(solution)/shard_map/while/body/eval_jaxpr/gather | solution.py:40
  332.1 6.2 multiply_reduce_fusion.3
  344.7 45.0 %gather_fusion = f32[12288,128]{1,0:T(8,128)} fusion(f32[17920,128]{1,0:T(8,128)} %get-tuple-element.206, s32[12288]{0:T(1024)S(1)} %broadcast_clamp_fusion.3), kind=kCustom, calls=%fused_computation.clone.1 | custom fusion | bytes 12632064 | tf_op jit(solution)/shard_map/while/body/eval_jaxpr/gather | solution.py:40
  389.6 6.2 multiply_reduce_fusion.3
  402.1 45.0 %gather_fusion = f32[12288,128]{1,0:T(8,128)} fusion(f32[17920,128]{1,0:T(8,128)} %get-tuple-element.206, s32[12288]{0:T(1024)S(1)} %broadcast_clamp_fusion.3), kind=kCustom, calls=%fused_computation.clone.1 | custom fusion | bytes 12632064 | tf_op jit(solution)/shard_map/while/body/eval_jaxpr/gather | solution.py:40
  447.1 6.2 multiply_reduce_fusion.3
  459.6 45.0 %gather_fusion = f32[12288,128]{1,0:T(8,128)} fusion(f32[17920,128]{1,0:T(8,128)} %get-tuple-element.206, s32[12288]{0:T(1024)S(1)} %broadcast_clamp_fusion.3), kind=kCustom, calls=%fused_computation.clone.1 | custom fusion | bytes 12632064 | tf_op jit(solution)/shard_map/while/body/eval_jaxpr/gather | solution.py:40
  504.6 6.2 multiply_reduce_fusion.3
  513.6 7.2 fusion.27
  520.8 5.4 gather_fusion.2
  536.4 27.6 %pad_maximum_fusion = bf16[17920,128]{1,0:T(8,128)(2,1)} fusion(bf16[512,128]{1,0:T(8,128)(2,1)S(1)} %collective-permute-done.4, bf16[512,128]{1,0:T(8,128)(2,1)S(1)} %collective-permute-done.3, bf16[512,128]{1,0:T(8,128)(2,1)S(1)} %collective-permute-done.2, bf16[16384,128]{1,0:T(8,128)(2,1)} %fusion.27), kind=kLoop, calls=%fused_computation.55 | loop fusion | flops 18350080 | bytes 9175040 | tf_op jit(solution)/shard_map/concatenate | solution.py:98
  564.0 58.3 %gather_fusion.4 = bf16[16384,128]{1,0:T(8,128)(2,1)} fusion(bf16[17920,128]{1,0:T(8,128)(2,1)} %pad_maximum_fusion, s32[16384]{0:T(1024)S(1)} %fusion.52), kind=kCustom, calls=%fused_computation.4 | custom fusion | bytes 8454144 | tf_op jit(solution)/shard_map/gather | solution.py:104
  622.3 10.4 %convert_reduce_fusion = f32[2048,128]{1,0:T(8,128)S(1)} fusion(bf16[16384,128]{1,0:T(8,128)(2,1)} %gather_fusion.4), kind=kLoop, calls=%fused_computation.41 | loop fusion | flops 3932160 | bytes 5242880 | tf_op jit(solution)/shard_map/reduce_sum | solution.py:103
  641.0 41.4 %gather_fusion.6 = f32[12288,128]{1,0:T(8,128)} fusion(f32[2816,128]{1,0:T(8,128)S(1)} %fusion.38, s32[12288]{0:T(1024)S(1)} %copy-done.1), kind=kCustom, calls=%fused_computation.6 | custom fusion | bytes 12632064 | tf_op jit(solution)/shard_map/while/body/eval_jaxpr/gather | solution.py:40
  682.3 6.4 multiply_reduce_fusion.1
  694.2 12.2 %collective-permute-done.10 = bf16[2048,128]{1,0:T(8,128)(2,1)S(1)} collective-permute-done((bf16[2048,128]{1,0:T(8,128)(2,1)S(1)}, bf16[2048,128]{1,0:T(8,128)(2,1)S(1)}, u32[]{:S(2)}, u32[]{:S(2)}) %collective-permute-start.10) | collective-permute-done | bytes 524320 | tf_op jit(solution)/shard_map/ppermute | solution.py:27
  706.5 10.8 %collective-permute-done.11 = bf16[2048,128]{1,0:T(8,128)(2,1)S(1)} collective-permute-done((bf16[2048,128]{1,0:T(8,128)(2,1)S(1)}, bf16[2048,128]{1,0:T(8,128)(2,1)S(1)}, u32[]{:S(2)}, u32[]{:S(2)}) %collective-permute-start.11) | collective-permute-done | bytes 524320 | tf_op jit(solution)/shard_map/ppermute | solution.py:27
  717.3 5.6 collective-permute-done.12
  723.0 63.0 %gather_fusion.7 = bf16[16384,128]{1,0:T(8,128)(2,1)} fusion(bf16[8192,128]{1,0:T(8,128)(2,1)S(1)} %pad_maximum_fusion.1, s32[16384]{0:T(1024)} %get-tuple-element.105), kind=kCustom, calls=%fused_computation.7 | custom fusion | bytes 8454144 | tf_op jit(solution)/shard_map/gather | solution.py:117
  (146 shorter events, 92.6 us)
Async XLA Ops:
  0.6 29.8 %copy-start.9 = (f32[2,2,128]{2,1,0:T(2,128)S(1)}, f32[2,2,128]{2,1,0:T(2,128)}, u32[]{:S(2)}) copy-start(f32[2,2,128]{2,1,0:T(2,128)} %param.19) | copy-start | bytes 6148
  0.6 30.4 %copy-start.10 = (s32[256]{0:T(256)S(1)}, s32[256]{0:T(256)}, u32[]{:S(2)}) copy-start(s32[256]{0:T(256)} %param.15) | copy-start | bytes 3076
  0.7 30.4 %copy-start.7 = (s32[6,2048]{1,0:T(8,128)S(1)}, s32[6,2048]{1,0:T(8,128)}, u32[]{:S(2)}) copy-start(s32[6,2048]{1,0:T(8,128)} %param.16) | copy-start | bytes 147460
  0.7 31.1 %copy-start.2 = (bf16[2,3,128,128]{3,2,1,0:T(8,128)(2,1)S(1)}, bf16[2,3,128,128]{3,2,1,0:T(8,128)(2,1)}, u32[]{:S(2)}) copy-start(bf16[2,3,128,128]{3,2,1,0:T(8,128)(2,1)} %param.17) | copy-start | bytes 589828
  0.7 31.0 %copy-start.4 = (bf16[2,3,128,128]{3,2,1,0:T(8,128)(2,1)S(1)}, bf16[2,3,128,128]{3,2,1,0:T(8,128)(2,1)}, u32[]{:S(2)}) copy-start(bf16[2,3,128,128]{3,2,1,0:T(8,128)(2,1)} %param.18) | copy-start | bytes 589828
  5.2 41.0 %collective-permute-start = (bf16[512,128]{1,0:T(8,128)(2,1)S(1)}, bf16[512,128]{1,0:T(8,128)(2,1)S(1)}, u32[]{:S(2)}, u32[]{:S(2)}) collective-permute-start(bf16[512,128]{1,0:T(8,128)(2,1)S(1)} %gather_fusion.1), channel_id=1, source_target_pairs={{0,1},{1,2},{2,3},{3,4},{4,5},{5,6},{6,7},{7,8},{8,9},{9,10},{10,1... | collective-permute-start | bytes 393224 | tf_op jit(solution)/shard_map/ppermute | solution.py:16
  5.7 40.5 %collective-permute-start.1 = (bf16[512,128]{1,0:T(8,128)(2,1)S(1)}, bf16[512,128]{1,0:T(8,128)(2,1)S(1)}, u32[]{:S(2)}, u32[]{:S(2)}) collective-permute-start(bf16[512,128]{1,0:T(8,128)(2,1)S(1)} %gather_fusion.1), channel_id=1, source_target_pairs={{1,0},{2,1},{3,2},{4,3},{5,4},{6,5},{7,6},{8,7},{9,8},{10,9},{11,1... | collective-permute-start | bytes 393224 | tf_op jit(solution)/shard_map/ppermute | solution.py:19
  20.1 14.8 %copy-start.5 = (s32[2048]{0:T(1024)}, s32[2048]{0:T(1024)S(1)}, u32[]{:S(2)}) copy-start(s32[2048]{0:T(1024)S(1)} %pad_clamp_fusion) | copy-start | bytes 24580
  28.5 5.8 collective-permute-start.5
  28.6 6.3 collective-permute-start.6
  28.7 6.3 collective-permute-start.7
  513.6 7.2 copy-start.6
  513.6 15.0 %copy-start.8 = (s32[17920]{0:T(1024)S(1)}, s32[17920]{0:T(1024)}, u32[]{:S(2)}) copy-start(s32[17920]{0:T(1024)} %get-tuple-element.77) | copy-start | bytes 215044
  526.2 7.1 collective-permute-start.2
  527.3 9.1 %collective-permute-start.3 = (bf16[512,128]{1,0:T(8,128)(2,1)S(1)}, bf16[512,128]{1,0:T(8,128)(2,1)S(1)}, u32[]{:S(2)}, u32[]{:S(2)}) collective-permute-start(bf16[512,128]{1,0:T(8,128)(2,1)S(1)} %get-tuple-element.101), channel_id=1, source_target_pairs={{14,0},{15,1},{0,2},{1,3},{2,4},{3,5},{4,6},{5,7},{6,8},{7,9},{8,1... | collective-permute-start | bytes 393224 | tf_op jit(solution)/shard_map/ppermute | solution.py:27
  527.3 9.1 %collective-permute-start.4 = (bf16[512,128]{1,0:T(8,128)(2,1)S(1)}, bf16[512,128]{1,0:T(8,128)(2,1)S(1)}, u32[]{:S(2)}, u32[]{:S(2)}) collective-permute-start(bf16[512,128]{1,0:T(8,128)(2,1)S(1)} %get-tuple-element.102), channel_id=1, source_target_pairs={{13,0},{14,1},{15,2},{0,3},{1,4},{2,5},{3,6},{4,7},{5,8},{6,9},{7,... | collective-permute-start | bytes 393224 | tf_op jit(solution)/shard_map/ppermute | solution.py:27
  622.3 16.0 %copy-start.3 = (bf16[2,3,128,128]{3,2,1,0:T(8,128)(2,1)S(1)}, bf16[2,3,128,128]{3,2,1,0:T(8,128)(2,1)}, u32[]{:S(2)}) copy-start(bf16[2,3,128,128]{3,2,1,0:T(8,128)(2,1)} %param.17) | copy-start | bytes 589828
  622.3 18.7 %copy-start.1 = (s32[12288]{0:T(1024)S(1)}, s32[12288]{0:T(1024)}, u32[]{:S(2)}) copy-start(s32[12288]{0:T(1024)} %broadcast_clamp_fusion.1) | copy-start | bytes 147460
  633.8 6.8 collective-permute-start.8
  636.2 4.4 collective-permute-start.9
  640.9 41.4 %copy-start.12 = (f32[128]{0:T(128)S(1)}, f32[128]{0:T(128)}, u32[]{:S(2)}) copy-start(f32[128]{0:T(128)} %get-tuple-element.110) | copy-start | bytes 1540
  682.3 6.4 copy-start.11
  690.1 96.0 %copy-start = (bf16[2048,128]{1,0:T(8,128)(2,1)}, bf16[2048,128]{1,0:T(8,128)(2,1)S(1)}, u32[]{:S(2)}) copy-start(bf16[2048,128]{1,0:T(8,128)(2,1)S(1)} %convolution_convert_fusion) | copy-start | bytes 1572868
  690.1 16.4 %collective-permute-start.10 = (bf16[2048,128]{1,0:T(8,128)(2,1)S(1)}, bf16[2048,128]{1,0:T(8,128)(2,1)S(1)}, u32[]{:S(2)}, u32[]{:S(2)}) collective-permute-start(bf16[2048,128]{1,0:T(8,128)(2,1)S(1)} %convolution_convert_fusion), channel_id=1, source_target_pairs={{1,0},{2,1},{3,2},{4,3},{5,4},{6,5},{7,6},{8,7},{9,8},{10,9},{11,1... | collective-permute-start | bytes 1572872 | tf_op jit(solution)/shard_map/ppermute | solution.py:27
  694.2 23.0 %collective-permute-start.11 = (bf16[2048,128]{1,0:T(8,128)(2,1)S(1)}, bf16[2048,128]{1,0:T(8,128)(2,1)S(1)}, u32[]{:S(2)}, u32[]{:S(2)}) collective-permute-start(bf16[2048,128]{1,0:T(8,128)(2,1)S(1)} %convolution_convert_fusion), channel_id=1, source_target_pairs={{2,0},{3,1},{4,2},{5,3},{6,4},{7,5},{8,6},{9,7},{10,8},{11,9},{12,... | collective-permute-start | bytes 1572872 | tf_op jit(solution)/shard_map/ppermute | solution.py:27
  694.2 28.7 %collective-permute-start.12 = (bf16[2048,128]{1,0:T(8,128)(2,1)S(1)}, bf16[2048,128]{1,0:T(8,128)(2,1)S(1)}, u32[]{:S(2)}, u32[]{:S(2)}) collective-permute-start(bf16[2048,128]{1,0:T(8,128)(2,1)S(1)} %convolution_convert_fusion), channel_id=1, source_target_pairs={{3,0},{4,1},{5,2},{6,3},{7,4},{8,5},{9,6},{10,7},{11,8},{12,9},{13... | collective-permute-start | bytes 1572872 | tf_op jit(solution)/shard_map/ppermute | solution.py:27
where the time goes:
time: 801 us; the launch traced here: 792 us
  local copies, waits for them, and re-layouts  547 us (68%)
  matrix products  100 us (12%)
  other arithmetic  80.3 us (10%)
  waiting for transfers between devices  39.1 us (5%)
  starting transfers between devices  18.4 us (2%)
    gather x9, local copies, waits for them, and re-layouts, one_block(): pre_act = own_term[None] + far_term[nbr_block] + bias_pair[0]  401 us
    gather x1, local copies, waits for them, and re-layouts, on_device(): lookup[combined_key].astype(jnp.float32)  63 us
    gather x1, local copies, waits for them, and re-layouts, on_device(): member_rows[grouped].reshape(coarse_rows, RATIO, width).astype(jnp.float32)  58.3 us
    dot_general x9, matrix products, one_block(): jnp.einsum('kbh,hg->kbg', hidden, edge_proj[2], preferred_element_type=jn...  55.8 us
    ppermute x9, waiting for transfers between devices, from_behind(): return lax.ppermute(block, axis, route)  39 us
    concatenate x1, other arithmetic, on_device(): member_rows = jnp.concatenate([fine_out] + arrived_rows, axis=0)  27.6 us
  transfers between devices with their start and end apart: 13, of which 7 were waited for; matrix products, arithmetic and copies ran while one was open for 4% of the time, Pallas kernels for 0%

commit v1 on v0

v1 whole, which is shorter than its diff:
```python
import functools

import jax
import jax.numpy as jnp
from jax import lax
from jax.experimental import pallas as pl
from jax.experimental.pallas import tpu as pltpu
from jax.sharding import PartitionSpec as P

RATIO = 8
REACH = 4
AXES = ("dom", "sub")
VMEM_LIMIT = 48 * 1024 * 1024
CHUNK = 64


def half_silu(half):
    return half + half * jnp.tanh(half)


def layer_kernel(
    degree, rows, keep, idx_ref, z_ref, far_ref, own_ref, mid_ref, mix_ref, last_ref, bias_ref, out_ref, even, odd
):
    count = rows // CHUNK

    def gather(chunk, target):
        base = chunk * CHUNK
        for k in range(degree):
            for j in range(CHUNK):
                r = k * CHUNK + j
                target[r : r + 1, :] = far_ref[idx_ref[base + (k * rows + j)]]

    def compute(chunk, source):
        start = pl.multiple_of(chunk * CHUNK, CHUNK)
        z = z_ref[pl.ds(start, CHUNK), :]
        both = jnp.dot(z, own_ref[...], preferred_element_type=jnp.float32)
        width = z.shape[1]
        own = 0.5 * (both[:, :width] + bias_ref[0:1, :])
        node = both[:, width:] + bias_ref[1:2, :]
        hidden = [
            half_silu(source[k * CHUNK : (k + 1) * CHUNK, :] + own).astype(jnp.bfloat16)
            for k in range(degree)
        ]
        msg = half_silu(
            0.5
            * jnp.dot(
                jnp.concatenate(hidden, axis=0), mid_ref[...], preferred_element_type=jnp.float32
            )
        )
        agg = msg[:CHUNK]
        for k in range(1, degree):
            agg = agg + msg[k * CHUNK : (k + 1) * CHUNK]
        pre = node + jnp.dot(
            agg.astype(jnp.bfloat16), mix_ref[...], preferred_element_type=jnp.float32
        )
        inner = half_silu(0.5 * pre).astype(jnp.bfloat16)
        update = jnp.dot(inner, last_ref[...], preferred_element_type=jnp.float32)
        if keep:
            update = (z.astype(jnp.float32) + update).astype(jnp.bfloat16)
        out_ref[pl.ds(start, CHUNK), :] = update.astype(out_ref.dtype)

    gather(0, even)

    def pair(p, carry):
        first = p * 2
        gather(first + 1, odd)
        compute(first, even)
        gather(jnp.minimum(first + 2, count - 1), even)
        compute(first + 1, odd)
        return carry

    lax.fori_loop(0, count // 2, pair, 0)


def message_layer(states, table, neighbor_idx, edge_proj, node_proj, bias_pair, keep):
    count_rows, width = states.shape
    degree = neighbor_idx.shape[0]
    rows = min(2048, count_rows)
    blocks = count_rows // rows
    far = 0.5 * jnp.dot(table, edge_proj[1], preferred_element_type=jnp.float32)
    far = far.reshape(table.shape[0], 1, width)
    order = neighbor_idx.reshape(degree, blocks, rows).transpose(1, 0, 2).reshape(-1)
    own = jnp.concatenate([edge_proj[0], node_proj[0]], axis=1)
    whole = pl.BlockSpec(memory_space=pltpu.VMEM)
    edges = count_rows * degree
    return pl.pallas_call(
        functools.partial(layer_kernel, degree, rows, keep),
        grid=(blocks,),
        in_specs=[
            pl.BlockSpec((degree * rows,), lambda i: (i,), memory_space=pltpu.SMEM),
            pl.BlockSpec((rows, width), lambda i: (i, 0)),
            whole,
            whole,
            whole,
            whole,
            whole,
            whole,
        ],
        out_specs=pl.BlockSpec((rows, width), lambda i: (i, 0)),
        out_shape=jax.ShapeDtypeStruct(
            (count_rows, width), jnp.float32 if keep else jnp.bfloat16
        ),
        scratch_shapes=[pltpu.VMEM((degree * CHUNK, width), jnp.float32)] * 2,
        compiler_params=pltpu.CompilerParams(vmem_limit_bytes=VMEM_LIMIT),
        cost_estimate=pl.CostEstimate(
            flops=2 * edges * width * width,
            bytes_accessed=table.shape[0] * width * 4 + count_rows * width * 6,
            transcendentals=2 * edges * width,
        ),
    )(order, states, far, own, edge_proj[2], node_proj[1], node_proj[2], bias_pair)


def pool_kernel(rows, idx_ref, own_ref, come_ref, out_ref, table, total, sems):
    @pl.when(pl.program_id(0) == 0)
    def _():
        near = own_ref.shape[0]
        first = pltpu.make_async_copy(own_ref, table.at[pl.ds(0, near)], sems.at[0])
        second = pltpu.make_async_copy(
            come_ref, table.at[pl.ds(near, come_ref.shape[0])], sems.at[1]
        )
        first.start()
        second.start()
        first.wait()
        second.wait()

    step = 32

    def some(c, carry):
        start = pl.multiple_of(c * step, step)
        for j in range(step):
            base = start * RATIO + j * RATIO
            parts = [table[idx_ref[base + k]] for k in range(RATIO)]
            while len(parts) > 1:
                parts = [a + b for a, b in zip(parts[::2], parts[1::2])]
            total[j : j + 1, :] = parts[0]
        out_ref[pl.ds(start, step), :] = (total[...] * (1.0 / RATIO)).astype(out_ref.dtype)
        return carry

    lax.fori_loop(0, rows // step, some, 0)


def pool(own, come, grouped, coarse_rows):
    width = own.shape[-1]
    rows = min(512, coarse_rows)
    return pl.pallas_call(
        functools.partial(pool_kernel, rows),
        grid=(coarse_rows // rows,),
        in_specs=[
            pl.BlockSpec((rows * RATIO,), lambda i: (i,), memory_space=pltpu.SMEM),
            pl.BlockSpec(memory_space=pl.ANY),
            pl.BlockSpec(memory_space=pl.ANY),
        ],
        out_specs=pl.BlockSpec((rows, width), lambda i: (i, 0)),
        out_shape=jax.ShapeDtypeStruct((coarse_rows, width), jnp.bfloat16),
        scratch_shapes=[
            pltpu.VMEM((own.shape[0] + come.shape[0], 1, width), jnp.float32),
            pltpu.VMEM((32, width), jnp.float32),
            pltpu.SemaphoreType.DMA((2,)),
        ],
        compiler_params=pltpu.CompilerParams(vmem_limit_bytes=VMEM_LIMIT),
    )(grouped, own, come)


def spread_kernel(rows, idx_ref, fine_ref, table_ref, out_ref, even):
    step = even.shape[0]

    def some(c, carry):
        start = pl.multiple_of(c * step, step)
        for j in range(step):
            even[j : j + 1, :] = table_ref[idx_ref[start + j]]
        out_ref[pl.ds(start, step), :] = (fine_ref[pl.ds(start, step), :] + even[...]).astype(
            out_ref.dtype
        )
        return carry

    lax.fori_loop(0, rows // step, some, 0)


def spread(fine, table, index):
    count_rows, width = fine.shape
    rows = min(2048, count_rows)
    return pl.pallas_call(
        functools.partial(spread_kernel, rows),
        grid=(count_rows // rows,),
        in_specs=[
            pl.BlockSpec((rows,), lambda i: (i,), memory_space=pltpu.SMEM),
            pl.BlockSpec((rows, width), lambda i: (i, 0)),
            pl.BlockSpec(memory_space=pltpu.VMEM),
        ],
        out_specs=pl.BlockSpec((rows, width), lambda i: (i, 0)),
        out_shape=jax.ShapeDtypeStruct((count_rows, width), jnp.bfloat16),
        scratch_shapes=[pltpu.VMEM((128, width), jnp.float32)],
        compiler_params=pltpu.CompilerParams(vmem_limit_bytes=VMEM_LIMIT),
    )(index, fine, table.reshape(table.shape[0], 1, width))


def from_behind(block, distance):
    count = lax.axis_size(AXES)
    return lax.ppermute(block, AXES, [((i - distance) % count, i) for i in range(count)])


def extended(table, block):
    return jnp.concatenate([table, from_behind(block, 1), block, from_behind(block, -1)], axis=0)


def on_device(
    features,
    fine_nbrs,
    send_rows,
    cluster,
    coarse_send,
    coarse_nbrs,
    edge_weights,
    node_weights,
    biases,
):
    local_rows, width = features.shape
    coarse_rows = local_rows // RATIO
    spill = local_rows // 32
    local_count = local_rows - (REACH - 1) * spill
    neighbor_table = extended(features, features[send_rows])

    num_parts = lax.axis_size(AXES)
    position = lax.axis_index(AXES)
    reach_index = (cluster // coarse_rows - position) % num_parts
    slot_index = cluster % coarse_rows
    combined = reach_index * coarse_rows + slot_index
    place = jnp.arange(local_rows, dtype=jnp.int32)
    ordering = lax.sort(reach_index * local_rows + place, is_stable=False)
    remote = ordering[local_count:] % local_rows
    leaving_slots = slot_index[remote]
    arrived_slots = [
        from_behind(leaving_slots[(d - 1) * spill : d * spill], d) for d in range(1, REACH)
    ]
    keys = jnp.concatenate(
        [jnp.where(reach_index == 0, slot_index, coarse_rows)] + arrived_slots, axis=0
    )
    members = 2 * local_rows
    grouped = lax.sort(
        keys * members + jnp.arange(keys.shape[0], dtype=jnp.int32), is_stable=False
    )[: coarse_rows * RATIO] % members

    fine_out = message_layer(
        features, neighbor_table, fine_nbrs, edge_weights[0], node_weights[0], biases[0], True
    )
    leaving_rows = fine_out[remote].astype(jnp.bfloat16)
    arrived_rows = jnp.concatenate(
        [from_behind(leaving_rows[(d - 1) * spill : d * spill], d) for d in range(1, REACH)], axis=0
    ).astype(jnp.float32)
    coarse_in = pool(
        fine_out.reshape(local_rows, 1, width),
        arrived_rows.reshape(-1, 1, width),
        grouped,
        coarse_rows,
    )
    coarse_table = extended(coarse_in, coarse_in[coarse_send])
    coarse_update = message_layer(
        coarse_in, coarse_table, coarse_nbrs, edge_weights[1], node_weights[1], biases[1], False
    )
    lookup = jnp.concatenate(
        [coarse_update] + [from_behind(coarse_update, -d) for d in range(1, REACH)], axis=0
    ).astype(jnp.float32)
    nodes = spread(fine_out, lookup, combined)
    return (nodes, coarse_update)


def solution(mesh):
    spread_over = ("groups", "dom", "sub")
    return jax.shard_map(
        on_device,
        mesh=mesh,
        in_specs=(
            P(spread_over, None),
            P(None, spread_over),
            P(spread_over),
            P(spread_over),
            P(spread_over),
            P(None, spread_over),
            P(),
            P(),
            P(),
        ),
        out_specs=(P(spread_over, None), P(spread_over, None)),
        check_vma=False,
    )
```

time: 801 us -> 437 us (0.55)
  local copies, waits for them, and re-layouts: 547 us -> 46.5 us
  Pallas kernels: 0 us -> 228 us
  matrix products: 100 us -> 30.4 us
  waiting for transfers between devices: 39.1 us -> 27.7 us
    gather x14 -> x3, local copies, waits for them, and re-layouts: 533 us -> 10.6 us  [the longest x1 6.01 us: on_device(): leaving_rows = fine_out[remote].astype(jnp.bfloat16)]
    pallas_call x0 -> x4, Pallas kernels: none -> 228 us  [the longest x2 193 us: message_layer(): pl.pallas_call(functools.partial(layer_kernel, degree, rows, keep), grid=...]
    dot_general x38 -> x2, matrix products: 100 us -> 30.4 us  [message_layer(): far = 0.5 * jnp.dot(table, edge_proj[1], preferred_element_type=jnp.float32)]
    convert_element_type x3 -> x2, other arithmetic: 12.6 us -> 60.8 us  [the longest x1 54.1 us: on_device(): lookup = jnp.concatenate([coarse_update] + [from_behind(coarse_update, -d...]
    concatenate x3 -> x2, other arithmetic: 27.7 us -> 0.02 us  [message_layer(): own = jnp.concatenate([edge_proj[0], node_proj[0]], axis=1)]
    concatenate x0 -> x7, local copies, waits for them, and re-layouts: none -> 27.2 us  [the longest x4 26.6 us: on_device(): jnp.concatenate([coarse_update] + [from_behind(coarse_update, -d) for d i...]
    ppermute x13, waiting for transfers between devices: 39.1 us -> 27.7 us  [from_behind(): lax.ppermute(block, AXES, [((i - distance) % count, i) for i in range(cou...]
    reduce_sum x1 -> x0, other arithmetic: 10.4 us -> none  [on_device(): jnp.sum(member_rows[grouped].reshape(coarse_rows, RATIO, width).astype(jn...]
  transfers between devices with their start and end apart: 13 -> 13, of which waited for: 7 -> 7; matrix products, arithmetic and copies ran while one was open for 4% -> 10% of each run, Pallas kernels for 0% -> 0%
where the time goes in v1:
time: 437 us; the launch traced here: 429 us
  Pallas kernels  228 us (52%)
  other arithmetic  77.5 us (18%)
  local copies, waits for them, and re-layouts  46.5 us (11%)
  matrix products  30.4 us (7%)
  waiting for transfers between devices  27.7 us (6%)
  starting transfers between devices  17.8 us (4%)
    pallas_call x2, Pallas kernels, message_layer(): pl.pallas_call(functools.partial(layer_kernel, degree, rows, keep), grid=...  193 us
    convert_element_type x1, other arithmetic, on_device(): lookup = jnp.concatenate([coarse_update] + [from_behind(coarse_update, -d...  54.1 us
    dot_general x2, matrix products, message_layer(): far = 0.5 * jnp.dot(table, edge_proj[1], preferred_element_type=jnp.float32)  30.4 us
    ppermute x13, waiting for transfers between devices, from_behind(): lax.ppermute(block, AXES, [((i - distance) % count, i) for i in range(cou...  27.7 us
    concatenate x4, local copies, waits for them, and re-layouts, on_device(): jnp.concatenate([coarse_update] + [from_behind(coarse_update, -d) for d i...  26.6 us
    ppermute x13, starting transfers between devices, from_behind(): lax.ppermute(block, AXES, [((i - distance) % count, i) for i in range(cou...  17.8 us
    pallas_call x1, Pallas kernels, pool(): pl.pallas_call(functools.partial(pool_kernel, rows), grid=(coarse_rows //...  17.8 us
    pallas_call x1, Pallas kernels, spread(): pl.pallas_call(functools.partial(spread_kernel, rows), grid=(count_rows /...  17.8 us
  transfers between devices with their start and end apart: 13, of which 7 were waited for; matrix products, arithmetic and copies ran while one was open for 10% of the time, Pallas kernels for 0%

profile of v1, /device:TPU:0, one launch (start us, length us, event | category | flops | bytes accessed | tf_op | source)
XLA Modules:
  0.0 429.5 jit_solution(7584140491305978984)
XLA Ops:
  0.6 0.7 compare_select_fusion.2
  1.3 3.8 gather_fusion
  5.6 5.0 %collective-permute-start.1 = (bf16[512,128]{1,0:T(8,128)(2,1)S(1)}, bf16[512,128]{1,0:T(8,128)(2,1)S(1)}, u32[]{:S(2)}, u32[]{:S(2)}) collective-permute-start(bf16[512,128]{1,0:T(8,128)(2,1)S(1)} %gather_fusion), channel_id=1, source_target_pairs={{1,0},{2,1},{3,2},{4,3},{5,4},{6,5},{7,6},{8,7},{9,8},{10,9},{11,1... | collective-permute-start | bytes 393224 | tf_op jit(solution)/shard_map/ppermute | solution.py:199
  10.6 0.9 compare_select_fusion
  11.6 6.3 %sort.14 = s32[16384]{0:T(1024)S(1)} sort(s32[16384]{0:T(1024)S(1)} %get-tuple-element.18), dimensions={0}, to_apply=%region_0.1 | sort | flops 229376 | bytes 131072 | tf_op jit(solution)/shard_map/sort | solution.py:229
  18.0 8.4 %gather_fusion.1 = s32[1536]{0:T(1024)S(1)} fusion(s32[16384]{0:T(1024)S(1)} %get-tuple-element.17, s32[2048]{0:T(1024)S(1)} %pad_clamp_fusion), kind=kCustom, calls=%fused_computation.1 | custom fusion | bytes 18432 | tf_op jit(solution)/shard_map/gather | solution.py:231
  26.5 1.6 collective-permute-start.4
  28.4 3.7 collective-permute-done.2
  32.8 8.7 %sort.15 = s32[17920]{0:T(1024)S(1)} sort(s32[17920]{0:T(1024)S(1)} %fusion.14), dimensions={0}, to_apply=%region_1.2 | sort | flops 268800 | bytes 143360 | tf_op jit(solution)/shard_map/sort | solution.py:239
  41.5 30.1 %convolution_multiply_fusion = f32[17920,128]{1,0:T(8,128)} fusion(bf16[512,128]{1,0:T(8,128)(2,1)S(1)} %collective-permute-done.1, bf16[512,128]{1,0:T(8,128)(2,1)S(1)} %gather_fusion, bf16[512,128]{1,0:T(8,128)(2,1)S(1)} %collective-permute-done, bf16[16384,128]{1,0:T(8,128)(2,1)} %z_ref.1, bf16[2,3,128,128]{3,2,1,0:T(8,128)(2,1)S(1)} %copy-done.3), kind=kOutput, calls=%fused_computation.4 | convolution fusion | flops 607846400 | bytes 13795328 | tf_op jit(solution)/shard_map/dot_general | solution.py:80
  71.6 170.0 %shard_map.104.fine_ref = f32[16384,128]{1,0:T(8,128)} custom-call(s32[98304]{0:T(1024)S(1)} %reshape.143.idx_ref, bf16[16384,128]{1,0:T(8,128)(2,1)S(1)} %copy-done, f32[17920,1,128]{2,1,0:T(1,128)} %bitcast.53, bf16[128,256]{1,0:T(8,128)(2,1)S(1)} %pad_maximum_fusion.own_ref, bf16[128,128]{1,0:T(8,128)(2,1)S(1)} %get-tuple-element.26.mid_ref, ...), custom_call_target="tpu_custom_call" | custom-call | flops 3221225472 | bytes 21757952 | tf_op jit(solution)/shard_map/pallas_call | solution.py:86
  241.6 6.0 %gather_fusion.2 = bf16[1536,128]{1,0:T(8,128)(2,1)S(1)} fusion(f32[16384,128]{1,0:T(8,128)} %shard_map.104.fine_ref, s32[2048]{0:T(1024)S(1)} %pad_clamp_fusion), kind=kCustom, calls=%fused_computation.2 | custom fusion | bytes 792576 | tf_op jit(solution)/shard_map/gather | solution.py:246
  247.7 0.9 collective-permute-start.5
  248.6 0.7 collective-permute-start.7
  249.3 5.5 %collective-permute-done.5 = bf16[512,128]{1,0:T(8,128)(2,1)S(1)} collective-permute-done((bf16[512,128]{1,0:T(8,128)(2,1)S(1)}, bf16[512,128]{1,0:T(8,128)(2,1)S(1)}, u32[]{:S(2)}, u32[]{:S(2)}) %collective-permute-start.5) | collective-permute-done | bytes 131104 | tf_op jit(solution)/shard_map/ppermute | solution.py:199
  255.0 2.7 collective-permute-done.6
  258.1 6.7 %maximum_convert_fusion.1.come_ref = f32[1536,1,128]{2,1,0:T(1,128)S(1)} fusion(bf16[512,1,128]{2,1,0:T(2,128)(2,1)S(1)} %copy.30, bf16[512,1,128]{2,1,0:T(2,128)(2,1)S(1)} %copy.29, bf16[512,1,128]{2,1,0:T(2,128)(2,1)S(1)} %copy.28), kind=kLoop, calls=%fused_computation.14 | loop fusion | flops 589824 | bytes 1179648 | tf_op jit(solution)/shard_map/convert_element_type | solution.py:249
  264.9 17.8 %shard_map.105.z_ref = bf16[2048,128]{1,0:T(8,128)(2,1)S(1)} custom-call(s32[16384]{0:T(1024)S(1)} %add_select_fusion.idx_ref, f32[16384,1,128]{2,1,0:T(1,128)} %bitcast.44, f32[1536,1,128]{2,1,0:T(1,128)S(1)} %maximum_convert_fusion.1.come_ref), custom_call_target="tpu_custom_call" | custom-call | tf_op jit(solution)/shard_map/pallas_call | solution.py:145
  282.6 0.9 gather_fusion.3
  283.5 2.4 collective-permute-start.8
  285.9 2.1 collective-permute-start.9
  288.0 1.9 collective-permute-done.8
  290.3 22.6 %shard_map.106 = bf16[2048,128]{1,0:T(8,128)(2,1)} custom-call(s32[12288]{0:T(1024)S(1)} %reshape_transpose_reshape.3.idx_ref, bf16[2048,128]{1,0:T(8,128)(2,1)S(1)} %shard_map.105.z_ref, f32[2816,1,128]{2,1,0:T(1,128)S(1)} %bitcast.43, bf16[128,256]{1,0:T(8,128)(2,1)S(1)} %pad_maximum_fusion.1.own_ref, bf16[128,128]{1,0:T(8,128)(2,1)S(1)} %get-tuple-element.27.mid_ref, ...), custom_call_target="tpu_custom_call" | custom-call | flops 402653184 | bytes 3014656 | tf_op jit(solution)/shard_map/pallas_call | solution.py:86
  312.9 4.4 %collective-permute-start.10 = (bf16[2048,128]{1,0:T(8,128)(2,1)}, bf16[2048,128]{1,0:T(8,128)(2,1)S(1)}, u32[]{:S(2)}, u32[]{:S(2)}) collective-permute-start(bf16[2048,128]{1,0:T(8,128)(2,1)} %shard_map.106), channel_id=1, source_target_pairs={{1,0},{2,1},{3,2},{4,3},{5,4},{6,5},{7,6},{8,7},{9,8},{10,9},{11,1... | collective-permute-start | bytes 1572872 | tf_op jit(solution)/shard_map/ppermute | solution.py:199
  317.3 2.0 copy.31
  319.3 10.6 %collective-permute-done.10 = bf16[2048,128]{1,0:T(8,128)(2,1)S(1)} collective-permute-done((bf16[2048,128]{1,0:T(8,128)(2,1)}, bf16[2048,128]{1,0:T(8,128)(2,1)S(1)}, u32[]{:S(2)}, u32[]{:S(2)}) %collective-permute-start.10) | collective-permute-done | bytes 524320 | tf_op jit(solution)/shard_map/ppermute | solution.py:199
  329.9 8.1 %copy.32 = bf16[2048,1,128]{2,1,0:T(2,128)(2,1)S(1)} copy(bf16[2048,1,128]{2,0,1:T(8,128)(2,1)S(1)} %bitcast.48) | data formatting | bytes 1048576 | tf_op jit(solution)/shard_map/concatenate | solution.py:260
  338.0 2.6 collective-permute-done.11
  340.7 8.1 %copy.33 = bf16[2048,1,128]{2,1,0:T(2,128)(2,1)S(1)} copy(bf16[2048,1,128]{2,0,1:T(8,128)(2,1)S(1)} %bitcast.47) | data formatting | bytes 1048576 | tf_op jit(solution)/shard_map/concatenate | solution.py:260
  348.8 8.4 %copy.34 = bf16[2048,1,128]{2,1,0:T(2,128)(2,1)S(1)} copy(bf16[2048,1,128]{2,0,1:T(8,128)(2,1)S(1)} %bitcast.46) | data formatting | bytes 1048576 | tf_op jit(solution)/shard_map/concatenate | solution.py:260
  357.2 54.1 %maximum_convert_fusion.table_ref = f32[8192,1,128]{2,1,0:T(1,128)S(1)} fusion(bf16[2048,1,128]{2,1,0:T(2,128)(2,1)S(1)} %copy.34, bf16[2048,1,128]{2,1,0:T(2,128)(2,1)S(1)} %copy.33, bf16[2048,1,128]{2,1,0:T(2,128)(2,1)S(1)} %copy.32, bf16[2048,1,128]{2,1,0:T(2,128)(2,1)S(1)} %copy.31), kind=kLoop, calls=%fused_computation.12 | loop fusion | flops 4194304 | bytes 6291456 | tf_op jit(solution)/shard_map/convert_element_type | solution.py:262
  411.3 17.8 %shard_map.107 = bf16[16384,128]{1,0:T(8,128)(2,1)} custom-call(s32[16384]{0:T(1024)S(1)} %get-tuple-element.16.idx_ref, f32[16384,128]{1,0:T(8,128)} %shard_map.104.fine_ref, f32[8192,1,128]{2,1,0:T(1,128)S(1)} %maximum_convert_fusion.table_ref), custom_call_target="tpu_custom_call" | custom-call | tf_op jit(solution)/shard_map/pallas_call | solution.py:182
  (46 shorter events, 2.6 us)
Async XLA Ops:
  5.1 36.4 %collective-permute-start = (bf16[512,128]{1,0:T(8,128)(2,1)S(1)}, bf16[512,128]{1,0:T(8,128)(2,1)S(1)}, u32[]{:S(2)}, u32[]{:S(2)}) collective-permute-start(bf16[512,128]{1,0:T(8,128)(2,1)S(1)} %gather_fusion), channel_id=1, source_target_pairs={{15,0},{0,1},{1,2},{2,3},{3,4},{4,5},{5,6},{6,7},{7,8},{8,9},{9,10... | collective-permute-start | bytes 393224 | tf_op jit(solution)/shard_map/ppermute | solution.py:199
  5.6 35.9 %collective-permute-start.1 = (bf16[512,128]{1,0:T(8,128)(2,1)S(1)}, bf16[512,128]{1,0:T(8,128)(2,1)S(1)}, u32[]{:S(2)}, u32[]{:S(2)}) collective-permute-start(bf16[512,128]{1,0:T(8,128)(2,1)S(1)} %gather_fusion), channel_id=1, source_target_pairs={{1,0},{2,1},{3,2},{4,3},{5,4},{6,5},{7,6},{8,7},{9,8},{10,9},{11,1... | collective-permute-start | bytes 393224 | tf_op jit(solution)/shard_map/ppermute | solution.py:199
  17.9 10.2 %copy-start.5 = (f32[2,2,128]{2,1,0:T(2,128)S(1)}, f32[2,2,128]{2,1,0:T(2,128)}, u32[]{:S(2)}) copy-start(f32[2,2,128]{2,1,0:T(2,128)} %param.17) | copy-start | bytes 6148
  17.9 10.2 %copy-start.6 = (s32[256]{0:T(256)S(1)}, s32[256]{0:T(256)}, u32[]{:S(2)}) copy-start(s32[256]{0:T(256)} %param.13) | copy-start | bytes 3076
  17.9 10.2 %copy-start.2 = (bf16[2,3,128,128]{3,2,1,0:T(8,128)(2,1)S(1)}, bf16[2,3,128,128]{3,2,1,0:T(8,128)(2,1)}, u32[]{:S(2)}) copy-start(bf16[2,3,128,128]{3,2,1,0:T(8,128)(2,1)} %param.16) | copy-start | bytes 589828
  17.9 10.2 %copy-start.3 = (bf16[2,3,128,128]{3,2,1,0:T(8,128)(2,1)S(1)}, bf16[2,3,128,128]{3,2,1,0:T(8,128)(2,1)}, u32[]{:S(2)}) copy-start(bf16[2,3,128,128]{3,2,1,0:T(8,128)(2,1)} %param.15) | copy-start | bytes 589828
  18.0 10.3 %copy-start.1 = (s32[6,16384]{1,0:T(8,128)S(1)}, s32[6,16384]{1,0:T(8,128)}, u32[]{:S(2)}) copy-start(s32[6,16384]{1,0:T(8,128)} %param.10) | copy-start | bytes 1179652
  18.0 10.4 %copy-start.4 = (s32[6,2048]{1,0:T(8,128)S(1)}, s32[6,2048]{1,0:T(8,128)}, u32[]{:S(2)}) copy-start(s32[6,2048]{1,0:T(8,128)} %param.14) | copy-start | bytes 147460
  26.4 5.8 %collective-permute-start.2 = (s32[512]{0:T(512)S(1)}, s32[512]{0:T(512)S(1)}, u32[]{:S(2)}, u32[]{:S(2)}) collective-permute-start(s32[512]{0:T(512)S(1)} %get-tuple-element.19), channel_id=1, source_target_pairs={{15,0},{0,1},{1,2},{2,3},{3,4},{4,5},{5,6},{6,7},{7,8},{8,9},{9,10... | collective-permute-start | bytes 6152 | tf_op jit(solution)/shard_map/ppermute | solution.py:199
  26.5 6.3 %collective-permute-start.3 = (s32[512]{0:T(512)S(1)}, s32[512]{0:T(512)S(1)}, u32[]{:S(2)}, u32[]{:S(2)}) collective-permute-start(s32[512]{0:T(512)S(1)} %get-tuple-element.20), channel_id=1, source_target_pairs={{14,0},{15,1},{0,2},{1,3},{2,4},{3,5},{4,6},{5,7},{6,8},{7,9},{8,1... | collective-permute-start | bytes 6152 | tf_op jit(solution)/shard_map/ppermute | solution.py:199
  26.5 6.3 %collective-permute-start.4 = (s32[512]{0:T(512)S(1)}, s32[512]{0:T(512)S(1)}, u32[]{:S(2)}, u32[]{:S(2)}) collective-permute-start(s32[512]{0:T(512)S(1)} %get-tuple-element.21), channel_id=1, source_target_pairs={{13,0},{14,1},{15,2},{0,3},{1,4},{2,5},{3,6},{4,7},{5,8},{6,9},{7,... | collective-permute-start | bytes 6152 | tf_op jit(solution)/shard_map/ppermute | solution.py:199
  41.5 30.1 %copy-start = (bf16[16384,128]{1,0:T(8,128)(2,1)S(1)}, bf16[16384,128]{1,0:T(8,128)(2,1)}, u32[]{:S(2)}) copy-start(bf16[16384,128]{1,0:T(8,128)(2,1)} %z_ref.1) | copy-start | bytes 12582916
  247.7 7.1 %collective-permute-start.5 = (bf16[512,128]{1,0:T(8,128)(2,1)S(1)}, bf16[512,128]{1,0:T(8,128)(2,1)S(1)}, u32[]{:S(2)}, u32[]{:S(2)}) collective-permute-start(bf16[512,128]{1,0:T(8,128)(2,1)S(1)} %get-tuple-element.2), channel_id=1, source_target_pairs={{15,0},{0,1},{1,2},{2,3},{3,4},{4,5},{5,6},{6,7},{7,8},{8,9},{9,10... | collective-permute-start | bytes 393224 | tf_op jit(solution)/shard_map/ppermute | solution.py:199
  248.6 9.1 %collective-permute-start.6 = (bf16[512,128]{1,0:T(8,128)(2,1)S(1)}, bf16[512,128]{1,0:T(8,128)(2,1)S(1)}, u32[]{:S(2)}, u32[]{:S(2)}) collective-permute-start(bf16[512,128]{1,0:T(8,128)(2,1)S(1)} %get-tuple-element.3), channel_id=1, source_target_pairs={{14,0},{15,1},{0,2},{1,3},{2,4},{3,5},{4,6},{5,7},{6,8},{7,9},{8,1... | collective-permute-start | bytes 393224 | tf_op jit(solution)/shard_map/ppermute | solution.py:199
  248.6 9.3 %collective-permute-start.7 = (bf16[512,128]{1,0:T(8,128)(2,1)S(1)}, bf16[512,128]{1,0:T(8,128)(2,1)S(1)}, u32[]{:S(2)}, u32[]{:S(2)}) collective-permute-start(bf16[512,128]{1,0:T(8,128)(2,1)S(1)} %get-tuple-element.4), channel_id=1, source_target_pairs={{13,0},{14,1},{15,2},{0,3},{1,4},{2,5},{3,6},{4,7},{5,8},{6,9},{7,... | collective-permute-start | bytes 393224 | tf_op jit(solution)/shard_map/ppermute | solution.py:199
  283.5 6.4 %collective-permute-start.8 = (bf16[256,128]{1,0:T(8,128)(2,1)S(1)}, bf16[256,128]{1,0:T(8,128)(2,1)S(1)}, u32[]{:S(2)}, u32[]{:S(2)}) collective-permute-start(bf16[256,128]{1,0:T(8,128)(2,1)S(1)} %gather_fusion.3), channel_id=1, source_target_pairs={{15,0},{0,1},{1,2},{2,3},{3,4},{4,5},{5,6},{6,7},{7,8},{8,9},{9,10... | collective-permute-start | bytes 196616 | tf_op jit(solution)/shard_map/ppermute | solution.py:199
  285.9 4.0 collective-permute-start.9
  312.9 17.0 %collective-permute-start.10 = (bf16[2048,128]{1,0:T(8,128)(2,1)}, bf16[2048,128]{1,0:T(8,128)(2,1)S(1)}, u32[]{:S(2)}, u32[]{:S(2)}) collective-permute-start(bf16[2048,128]{1,0:T(8,128)(2,1)} %shard_map.106), channel_id=1, source_target_pairs={{1,0},{2,1},{3,2},{4,3},{5,4},{6,5},{7,6},{8,7},{9,8},{10,9},{11,1... | collective-permute-start | bytes 1572872 | tf_op jit(solution)/shard_map/ppermute | solution.py:199
  317.3 23.3 %collective-permute-start.11 = (bf16[2048,128]{1,0:T(8,128)(2,1)}, bf16[2048,128]{1,0:T(8,128)(2,1)S(1)}, u32[]{:S(2)}, u32[]{:S(2)}) collective-permute-start(bf16[2048,128]{1,0:T(8,128)(2,1)} %shard_map.106), channel_id=1, source_target_pairs={{2,0},{3,1},{4,2},{5,3},{6,4},{7,5},{8,6},{9,7},{10,8},{11,9},{12,... | collective-permute-start | bytes 1572872 | tf_op jit(solution)/shard_map/ppermute | solution.py:199
  317.3 31.4 %collective-permute-start.12 = (bf16[2048,128]{1,0:T(8,128)(2,1)}, bf16[2048,128]{1,0:T(8,128)(2,1)S(1)}, u32[]{:S(2)}, u32[]{:S(2)}) collective-permute-start(bf16[2048,128]{1,0:T(8,128)(2,1)} %shard_map.106), channel_id=1, source_target_pairs={{3,0},{4,1},{5,2},{6,3},{7,4},{8,5},{9,6},{10,7},{11,8},{12,9},{13... | collective-permute-start | bytes 1572872 | tf_op jit(solution)/shard_map/ppermute | solution.py:199

commit v2 on v1

--- a/solution.py
+++ b/solution.py
@@ -11,7 +11,7 @@
 REACH = 4
 AXES = ("dom", "sub")
 VMEM_LIMIT = 48 * 1024 * 1024
-CHUNK = 64
+CHUNK = 128
 
 
 def half_silu(half):
@@ -19,37 +19,34 @@
 
 
 def layer_kernel(
-    degree, rows, keep, idx_ref, z_ref, far_ref, own_ref, mid_ref, mix_ref, last_ref, bias_ref, out_ref, even, odd
+    degree, rows, keep, idx_ref, z_ref, far_ref, own_ref, mid_ref, mix_ref, last_ref, bias_ref, out_ref, *rest
 ):
+    rounded_ref = None if keep else rest[0]
+    even, odd = rest[-2:]
     count = rows // CHUNK
 
-    def gather(chunk, target):
+    def gather(chunk, target, degrees=range(degree)):
         base = chunk * CHUNK
-        for k in range(degree):
+        for k in degrees:
             for j in range(CHUNK):
                 r = k * CHUNK + j
                 target[r : r + 1, :] = far_ref[idx_ref[base + (k * rows + j)]]
 
-    def compute(chunk, source):
+    def compute(chunk, source, following, target):
         start = pl.multiple_of(chunk * CHUNK, CHUNK)
         z = z_ref[pl.ds(start, CHUNK), :]
         both = jnp.dot(z, own_ref[...], preferred_element_type=jnp.float32)
         width = z.shape[1]
         own = 0.5 * (both[:, :width] + bias_ref[0:1, :])
         node = both[:, width:] + bias_ref[1:2, :]
-        hidden = [
-            half_silu(source[k * CHUNK : (k + 1) * CHUNK, :] + own).astype(jnp.bfloat16)
-            for k in range(degree)
-        ]
-        msg = half_silu(
-            0.5
-            * jnp.dot(
-                jnp.concatenate(hidden, axis=0), mid_ref[...], preferred_element_type=jnp.float32
+        agg = None
+        for k in range(degree):
+            gather(following, target, (k,))
+            hidden = half_silu(source[k * CHUNK : (k + 1) * CHUNK, :] + own).astype(jnp.bfloat16)
+            msg = half_silu(
+                0.5 * jnp.dot(hidden, mid_ref[...], preferred_element_type=jnp.float32)
             )
-        )
-        agg = msg[:CHUNK]
-        for k in range(1, degree):
-            agg = agg + msg[k * CHUNK : (k + 1) * CHUNK]
+            agg = msg if agg is None else agg + msg
         pre = node + jnp.dot(
             agg.astype(jnp.bfloat16), mix_ref[...], preferred_element_type=jnp.float32
         )
@@ -57,19 +54,24 @@
         update = jnp.dot(inner, last_ref[...], preferred_element_type=jnp.float32)
         if keep:
             update = (z.astype(jnp.float32) + update).astype(jnp.bfloat16)
-        out_ref[pl.ds(start, CHUNK), :] = update.astype(out_ref.dtype)
+        else:
+            rounded_ref[pl.ds(start, CHUNK), :] = update.astype(jnp.bfloat16)
+            update = update.astype(jnp.bfloat16)
+        out_ref[pl.ds(start, CHUNK), :] = update.astype(jnp.float32)
 
     gather(0, even)
 
     def pair(p, carry):
         first = p * 2
-        gather(first + 1, odd)
-        compute(first, even)
-        gather(jnp.minimum(first + 2, count - 1), even)
-        compute(first + 1, odd)
+        compute(first, even, first + 1, odd)
+        compute(first + 1, odd, jnp.minimum(first + 2, count - 1), even)
         return carry
 
     lax.fori_loop(0, count // 2, pair, 0)
+
+
+def by_row(table):
+    return lax.optimization_barrier(table).reshape(table.shape[0], 1, table.shape[1])
 
 
 def message_layer(states, table, neighbor_idx, edge_proj, node_proj, bias_pair, keep):
@@ -78,11 +80,12 @@
     rows = min(2048, count_rows)
     blocks = count_rows // rows
     far = 0.5 * jnp.dot(table, edge_proj[1], preferred_element_type=jnp.float32)
-    far = far.reshape(table.shape[0], 1, width)
+    far = by_row(far)
     order = neighbor_idx.reshape(degree, blocks, rows).transpose(1, 0, 2).reshape(-1)
     own = jnp.concatenate([edge_proj[0], node_proj[0]], axis=1)
     whole = pl.BlockSpec(memory_space=pltpu.VMEM)
     edges = count_rows * degree
+    kinds = (jnp.float32,) if keep else (jnp.float32, jnp.bfloat16)
     return pl.pallas_call(
         functools.partial(layer_kernel, degree, rows, keep),
         grid=(blocks,),
@@ -96,10 +99,8 @@
             whole,
             whole,
         ],
-        out_specs=pl.BlockSpec((rows, width), lambda i: (i, 0)),
-        out_shape=jax.ShapeDtypeStruct(
-            (count_rows, width), jnp.float32 if keep else jnp.bfloat16
-        ),
+        out_specs=[pl.BlockSpec((rows, width), lambda i: (i, 0))] * len(kinds),
+        out_shape=[jax.ShapeDtypeStruct((count_rows, width), kind) for kind in kinds],
         scratch_shapes=[pltpu.VMEM((degree * CHUNK, width), jnp.float32)] * 2,
         compiler_params=pltpu.CompilerParams(vmem_limit_bytes=VMEM_LIMIT),
         cost_estimate=pl.CostEstimate(
@@ -161,13 +162,22 @@
     )(grouped, own, come)
 
 
-def spread_kernel(rows, idx_ref, fine_ref, table_ref, out_ref, even):
+def spread_kernel(rows, near, far, idx_ref, fine_ref, own_ref, come_ref, out_ref, table, even, sems):
+    @pl.when(pl.program_id(0) == 0)
+    def _():
+        first = pltpu.make_async_copy(own_ref, table.at[pl.ds(0, near)], sems.at[0])
+        second = pltpu.make_async_copy(come_ref, table.at[pl.ds(near, far)], sems.at[1])
+        first.start()
+        second.start()
+        first.wait()
+        second.wait()
+
     step = even.shape[0]
 
     def some(c, carry):
         start = pl.multiple_of(c * step, step)
         for j in range(step):
-            even[j : j + 1, :] = table_ref[idx_ref[start + j]]
+            even[j : j + 1, :] = table[idx_ref[start + j]]
         out_ref[pl.ds(start, step), :] = (fine_ref[pl.ds(start, step), :] + even[...]).astype(
             out_ref.dtype
         )
@@ -176,22 +186,42 @@
     lax.fori_loop(0, rows // step, some, 0)
 
 
-def spread(fine, table, index):
+def spread(fine, own, come, index):
     count_rows, width = fine.shape
     rows = min(2048, count_rows)
+    near, far = own.shape[0], come.shape[0]
     return pl.pallas_call(
-        functools.partial(spread_kernel, rows),
+        functools.partial(spread_kernel, rows, near, far),
         grid=(count_rows // rows,),
         in_specs=[
             pl.BlockSpec((rows,), lambda i: (i,), memory_space=pltpu.SMEM),
             pl.BlockSpec((rows, width), lambda i: (i, 0)),
-            pl.BlockSpec(memory_space=pltpu.VMEM),
+            pl.BlockSpec(memory_space=pl.ANY),
+            pl.BlockSpec(memory_space=pl.ANY),
         ],
         out_specs=pl.BlockSpec((rows, width), lambda i: (i, 0)),
         out_shape=jax.ShapeDtypeStruct((count_rows, width), jnp.bfloat16),
-        scratch_shapes=[pltpu.VMEM((128, width), jnp.float32)],
+        scratch_shapes=[
+            pltpu.VMEM((near + far, 1, width), jnp.float32),
+            pltpu.VMEM((128, width), jnp.float32),
+            pltpu.SemaphoreType.DMA((2,)),
+        ],
         compiler_params=pltpu.CompilerParams(vmem_limit_bytes=VMEM_LIMIT),
-    )(index, fine, table.reshape(table.shape[0], 1, width))
+    )(index, fine, own, come)
+
+
+def ranks(reach_index):
+    lanes = 128
+    hit = (reach_index[None] == jnp.arange(1, REACH, dtype=jnp.int32)[:, None]).astype(jnp.bfloat16)
+    hit = hit.reshape(REACH - 1, -1, lanes)
+    lines = hit.shape[1]
+    before = jnp.triu(jnp.ones((lanes, lanes), jnp.bfloat16), 1)
+    above = jnp.tril(jnp.ones((lines, lines), jnp.bfloat16), -1)
+    inside = jnp.einsum("dri,ij->drj", hit, before, preferred_element_type=jnp.float32)
+    sums = jnp.sum(hit.astype(jnp.float32), axis=2).astype(jnp.bfloat16)
+    ahead = jnp.einsum("rs,ds->dr", above, sums, preferred_element_type=jnp.float32)
+    rank = (inside + ahead[:, :, None]) * hit.astype(jnp.float32)
+    return jnp.sum(rank, axis=0).reshape(-1).astype(jnp.int32)
 
 
 def from_behind(block, distance):
@@ -224,11 +254,18 @@
     position = lax.axis_index(AXES)
     reach_index = (cluster // coarse_rows - position) % num_parts
     slot_index = cluster % coarse_rows
-    combined = reach_index * coarse_rows + slot_index
+    wanted = jnp.where(
+        reach_index == 0,
+        slot_index,
+        coarse_rows + (reach_index - 1) * spill + ranks(reach_index),
+    )
     place = jnp.arange(local_rows, dtype=jnp.int32)
-    ordering = lax.sort(reach_index * local_rows + place, is_stable=False)
-    remote = ordering[local_count:] % local_rows
-    leaving_slots = slot_index[remote]
+    ordering = lax.sort(
+        (reach_index * local_rows + place) * coarse_rows + slot_index, is_stable=False
+    )
+    leaving = ordering[local_count:]
+    remote = leaving // coarse_rows % local_rows
+    leaving_slots = leaving % coarse_rows
     arrived_slots = [
         from_behind(leaving_slots[(d - 1) * spill : d * spill], d) for d in range(1, REACH)
     ]
@@ -240,27 +277,23 @@
         keys * members + jnp.arange(keys.shape[0], dtype=jnp.int32), is_stable=False
     )[: coarse_rows * RATIO] % members
 
-    fine_out = message_layer(
+    (fine_out,) = message_layer(
         features, neighbor_table, fine_nbrs, edge_weights[0], node_weights[0], biases[0], True
     )
     leaving_rows = fine_out[remote].astype(jnp.bfloat16)
     arrived_rows = jnp.concatenate(
         [from_behind(leaving_rows[(d - 1) * spill : d * spill], d) for d in range(1, REACH)], axis=0
     ).astype(jnp.float32)
-    coarse_in = pool(
-        fine_out.reshape(local_rows, 1, width),
-        arrived_rows.reshape(-1, 1, width),
-        grouped,
-        coarse_rows,
-    )
+    coarse_in = pool(by_row(fine_out), by_row(arrived_rows), grouped, coarse_rows)
     coarse_table = extended(coarse_in, coarse_in[coarse_send])
-    coarse_update = message_layer(
+    coarse_float, coarse_update = message_layer(
         coarse_in, coarse_table, coarse_nbrs, edge_weights[1], node_weights[1], biases[1], False
     )
-    lookup = jnp.concatenate(
-        [coarse_update] + [from_behind(coarse_update, -d) for d in range(1, REACH)], axis=0
+    answers = coarse_update[jnp.concatenate(arrived_slots)]
+    returned = jnp.concatenate(
+        [from_behind(answers[(d - 1) * spill : d * spill], -d) for d in range(1, REACH)], axis=0
     ).astype(jnp.float32)
-    nodes = spread(fine_out, lookup, combined)
+    nodes = spread(fine_out, by_row(coarse_float), by_row(returned), wanted)
     return (nodes, coarse_update)
 
 

time: 437 us -> 290 us (0.66); the launches traced: 429 us -> 289 us
  other arithmetic: 77.5 us -> 18.6 us
  Pallas kernels: 228 us -> 184 us
  local copies, waits for them, and re-layouts: 46.5 us -> 18.9 us
  waiting for transfers between devices: 27.7 us -> 13.7 us
    convert_element_type x1, other arithmetic: 54.1 us -> 0.05 us  [on_device(): returned = jnp.concatenate([from_behind(answers[(d - 1) * spill:d * spill...]
    pallas_call x2, Pallas kernels: 193 us -> 148 us  [message_layer(): pl.pallas_call(functools.partial(layer_kernel, degree, rows, keep), grid=...]
    concatenate x7 -> x0, local copies, waits for them, and re-layouts: 27.2 us -> none  [the longest x4 26.6 us: on_device(): jnp.concatenate([coarse_update] + [from_behind(coarse_update, -d) for d i...]
    ppermute x13, waiting for transfers between devices: 27.7 us -> 13.7 us  [from_behind(): lax.ppermute(block, AXES, [((i - distance) % count, i) for i in range(cou...]
    convert_element_type x1, other arithmetic: 6.73 us -> 0.05 us  [on_device(): arrived_rows = jnp.concatenate([from_behind(leaving_rows[(d - 1) * spill:...]
    gather x1, local copies, waits for them, and re-layouts: 8.39 us -> 3.74 us  [on_device(): answers = coarse_update[jnp.concatenate(arrived_slots)]]
  transfers between devices with their start and end apart: 13 -> 13, of which waited for: 7 -> 6; matrix products, arithmetic and copies ran while one was open for 10% -> 8% of each run, Pallas kernels for 0% -> 0%
where the time goes in v2:
time: 290 us; the launch traced here: 289 us
  Pallas kernels  184 us (63%)
  matrix products  31.2 us (11%)
  starting transfers between devices  21.2 us (7%)
  local copies, waits for them, and re-layouts  18.9 us (7%)
  other arithmetic  18.6 us (6%)
  waiting for transfers between devices  13.7 us (5%)
    pallas_call x2, Pallas kernels, message_layer(): pl.pallas_call(functools.partial(layer_kernel, degree, rows, keep), grid=...  148 us
    dot_general x2, matrix products, message_layer(): far = 0.5 * jnp.dot(table, edge_proj[1], preferred_element_type=jnp.float32)  30.8 us
    ppermute x13, starting transfers between devices, from_behind(): lax.ppermute(block, AXES, [((i - distance) % count, i) for i in range(cou...  21.2 us
    pallas_call x1, Pallas kernels, spread(): pl.pallas_call(functools.partial(spread_kernel, rows, near, far), grid=(c...  17.9 us
    pallas_call x1, Pallas kernels, pool(): pl.pallas_call(functools.partial(pool_kernel, rows), grid=(coarse_rows //...  17.8 us
    ppermute x13, waiting for transfers between devices, from_behind(): lax.ppermute(block, AXES, [((i - distance) % count, i) for i in range(cou...  13.7 us
    sort x1, other arithmetic, on_device(): lax.sort(keys * members + jnp.arange(keys.shape[0], dtype=jnp.int32), is_...  8.68 us
    sort x1, other arithmetic, on_device(): lax.sort((reach_index * local_rows + place) * coarse_rows + slot_index, i...  6.28 us
  transfers between devices with their start and end apart: 13, of which 6 were waited for; matrix products, arithmetic and copies ran while one was open for 8% of the time, Pallas kernels for 0%

profile of v2, /device:TPU:0, one launch (start us, length us, event | category | flops | bytes accessed | tf_op | source)
XLA Modules:
  0.0 288.7 jit_solution(5593792680328526736)
XLA Ops:
  1.3 3.8 %gather_fusion = bf16[512,128]{1,0:T(8,128)(2,1)S(1)} fusion(bf16[16384,128]{1,0:T(8,128)(2,1)} %z_ref.1, s32[1024]{0:T(1024)S(1)} %pad_clamp_fusion.3), kind=kCustom, calls=%fused_computation | custom fusion | bytes 264192 | tf_op jit(solution)/shard_map/gather | solution.py:251
  5.6 5.0 %collective-permute-start.1 = (bf16[512,128]{1,0:T(8,128)(2,1)S(1)}, bf16[512,128]{1,0:T(8,128)(2,1)S(1)}, u32[]{:S(2)}, u32[]{:S(2)}) collective-permute-start(bf16[512,128]{1,0:T(8,128)(2,1)S(1)} %gather_fusion), channel_id=1, source_target_pairs={{1,0},{2,1},{3,2},{4,3},{5,4},{6,5},{7,6},{8,7},{9,8},{10,9},{11,1... | collective-permute-start | bytes 393224 | tf_op jit(solution)/shard_map/ppermute | solution.py:229
  10.7 0.9 fusion.52
  12.2 1.0 broadcast_select_fusion
  13.2 6.3 %sort.14 = s32[16384]{0:T(1024)S(1)} sort(s32[16384]{0:T(1024)S(1)} %get-tuple-element.25), dimensions={0}, to_apply=%region_2.3 | sort | flops 229376 | bytes 131072 | tf_op jit(solution)/shard_map/sort | solution.py:263
  19.6 1.6 collective-permute-start.4
  21.2 0.9 slice_bitcast_fusion
  22.1 0.8 slice_bitcast_fusion.2
  22.9 0.7 slice_bitcast_fusion.10
  24.4 1.2 reshape.201.idx_ref
  25.5 0.9 reshape_transpose_reshape.3.idx_ref
  26.4 8.7 %sort.15 = s32[17920]{0:T(1024)S(1)} sort(s32[17920]{0:T(1024)S(1)} %fusion.20), dimensions={0}, to_apply=%region_3.4 | sort | flops 268800 | bytes 143360 | tf_op jit(solution)/shard_map/sort | solution.py:276
  35.1 29.7 %convolution_multiply_fusion = f32[17920,128]{1,0:T(8,128)} fusion(bf16[512,128]{1,0:T(8,128)(2,1)S(1)} %collective-permute-done.1, bf16[512,128]{1,0:T(8,128)(2,1)S(1)} %gather_fusion, bf16[512,128]{1,0:T(8,128)(2,1)S(1)} %collective-permute-done, bf16[16384,128]{1,0:T(8,128)(2,1)} %z_ref.1, bf16[2,3,128,128]{3,2,1,0:T(8,128)(2,1)} %param.15), kind=kOutput, calls=%fused_computation.4 | convolution fusion | flops 607846400 | bytes 13795328 | tf_op jit(solution)/shard_map/dot_general | solution.py:82
  64.8 130.9 %shard_map.104.fine_ref = f32[16384,128]{1,0:T(8,128)} custom-call(s32[98304]{0:T(1024)S(1)} %reshape.201.idx_ref, bf16[16384,128]{1,0:T(8,128)(2,1)S(1)} %copy-done, f32[17920,1,128]{2,1,0:T(1,128)} %bitcast.61, bf16[128,256]{1,0:T(8,128)(2,1)S(1)} %get-tuple-element.32.own_ref, bf16[128,128]{1,0:T(8,128)(2,1)S(1)} %get-tuple-element.21.mid_ref, ...), custom_call_target="tpu_custom_call" | custom-call | flops 3221225472 | bytes 21757952 | tf_op jit(solution)/shard_map/pallas_call | solution.py:89
  195.7 6.0 %gather_fusion.1 = bf16[1536,128]{1,0:T(8,128)(2,1)S(1)} fusion(f32[16384,128]{1,0:T(8,128)} %shard_map.104.fine_ref, s32[2048]{0:T(1024)S(1)} %pad_clamp_fusion.1), kind=kCustom, calls=%fused_computation.1 | custom fusion | bytes 792576 | tf_op jit(solution)/shard_map/gather | solution.py:283
  202.2 2.2 collective-permute-start.6
  204.3 2.4 collective-permute-start.7
  206.8 2.6 collective-permute-done.5
  209.4 1.5 collective-permute-done.6
  211.0 17.8 %shard_map.105.z_ref = bf16[2048,128]{1,0:T(8,128)(2,1)S(1)} custom-call(s32[16384]{0:T(1024)S(1)} %add_select_fusion.idx_ref, f32[16384,1,128]{2,1,0:T(1,128)} %bitcast.56, f32[1536,1,128]{2,1,0:T(1,128)S(1)} %bitcast.53), custom_call_target="tpu_custom_call" | custom-call | tf_op jit(solution)/shard_map/pallas_call | solution.py:146
  228.8 0.9 gather_fusion.2
  229.6 2.7 collective-permute-start.8
  232.3 1.8 collective-permute-start.9
  234.1 1.9 collective-permute-done.8
  236.1 1.1 convolution_multiply_fusion.1
  237.2 17.5 %shard_map.106 = (f32[2048,128]{1,0:T(8,128)S(1)}, bf16[2048,128]{1,0:T(8,128)(2,1)}) custom-call(s32[12288]{0:T(1024)S(1)} %reshape_transpose_reshape.3.idx_ref, bf16[2048,128]{1,0:T(8,128)(2,1)S(1)} %shard_map.105.z_ref, f32[2816,1,128]{2,1,0:T(1,128)S(1)} %bitcast.55, bf16[128,256]{1,0:T(8,128)(2,1)S(1)} %get-tuple-element.33.own_ref, ...), custom_call_target="tpu_custom_call" | custom-call | flops 402653184 | bytes 3014656 | tf_op jit(solution)/shard_map/pallas_call | solution.py:89
  254.7 3.7 %gather_fusion.3 = bf16[1536,128]{1,0:T(8,128)(2,1)S(1)} fusion(bf16[2048,128]{1,0:T(8,128)(2,1)} %get-tuple-element.3, s32[2048]{0:T(1024)S(1)} %pad_clamp_fusion), kind=kCustom, calls=%fused_computation.3 | custom fusion | bytes 792576 | tf_op jit(solution)/shard_map/gather | solution.py:292
  258.5 4.5 %collective-permute-start.10 = (bf16[512,128]{1,0:T(8,128)(2,1)S(1)}, bf16[512,128]{1,0:T(8,128)(2,1)S(1)}, u32[]{:S(2)}, u32[]{:S(2)}) collective-permute-start(bf16[512,128]{1,0:T(8,128)(2,1)S(1)} %get-tuple-element.8), channel_id=1, source_target_pairs={{1,0},{2,1},{3,2},{4,3},{5,4},{6,5},{7,6},{8,7},{9,8},{10,9},{11,1... | collective-permute-start | bytes 393224 | tf_op jit(solution)/shard_map/ppermute | solution.py:229
  263.0 3.8 %collective-permute-done.10 = bf16[512,128]{1,0:T(8,128)(2,1)S(1)} collective-permute-done((bf16[512,128]{1,0:T(8,128)(2,1)S(1)}, bf16[512,128]{1,0:T(8,128)(2,1)S(1)}, u32[]{:S(2)}, u32[]{:S(2)}) %collective-permute-start.10) | collective-permute-done | bytes 131104 | tf_op jit(solution)/shard_map/ppermute | solution.py:229
  266.8 2.4 collective-permute-done.11
  269.2 1.4 collective-permute-done.12
  270.7 17.9 %shard_map.107 = bf16[16384,128]{1,0:T(8,128)(2,1)} custom-call(s32[16384]{0:T(1024)S(1)} %get-tuple-element.26.idx_ref, f32[16384,128]{1,0:T(8,128)} %shard_map.104.fine_ref, f32[2048,1,128]{2,1,0:T(1,128)S(1)} %bitcast.54, f32[1536,1,128]{2,1,0:T(1,128)S(1)} %bitcast.52), custom_call_target="tpu_custom_call" | custom-call | tf_op jit(solution)/shard_map/pallas_call | solution.py:193
  (37 shorter events, 3.4 us)
Async XLA Ops:
  5.1 30.0 %collective-permute-start = (bf16[512,128]{1,0:T(8,128)(2,1)S(1)}, bf16[512,128]{1,0:T(8,128)(2,1)S(1)}, u32[]{:S(2)}, u32[]{:S(2)}) collective-permute-start(bf16[512,128]{1,0:T(8,128)(2,1)S(1)} %gather_fusion), channel_id=1, source_target_pairs={{15,0},{0,1},{1,2},{2,3},{3,4},{4,5},{5,6},{6,7},{7,8},{8,9},{9,10... | collective-permute-start | bytes 393224 | tf_op jit(solution)/shard_map/ppermute | solution.py:229
  5.6 29.5 %collective-permute-start.1 = (bf16[512,128]{1,0:T(8,128)(2,1)S(1)}, bf16[512,128]{1,0:T(8,128)(2,1)S(1)}, u32[]{:S(2)}, u32[]{:S(2)}) collective-permute-start(bf16[512,128]{1,0:T(8,128)(2,1)S(1)} %gather_fusion), channel_id=1, source_target_pairs={{1,0},{2,1},{3,2},{4,3},{5,4},{6,5},{7,6},{8,7},{9,8},{10,9},{11,1... | collective-permute-start | bytes 393224 | tf_op jit(solution)/shard_map/ppermute | solution.py:229
  19.5 6.9 %collective-permute-start.2 = (s32[512]{0:T(512)S(1)}, s32[512]{0:T(512)S(1)}, u32[]{:S(2)}, u32[]{:S(2)}) collective-permute-start(s32[512]{0:T(512)S(1)} %get-tuple-element.27), channel_id=1, source_target_pairs={{15,0},{0,1},{1,2},{2,3},{3,4},{4,5},{5,6},{6,7},{7,8},{8,9},{9,10... | collective-permute-start | bytes 6152 | tf_op jit(solution)/shard_map/ppermute | solution.py:229
  19.6 6.8 %collective-permute-start.3 = (s32[512]{0:T(512)S(1)}, s32[512]{0:T(512)S(1)}, u32[]{:S(2)}, u32[]{:S(2)}) collective-permute-start(s32[512]{0:T(512)S(1)} %get-tuple-element.29), channel_id=1, source_target_pairs={{14,0},{15,1},{0,2},{1,3},{2,4},{3,5},{4,6},{5,7},{6,8},{7,9},{8,1... | collective-permute-start | bytes 6152 | tf_op jit(solution)/shard_map/ppermute | solution.py:229
  19.6 6.8 %collective-permute-start.4 = (s32[512]{0:T(512)S(1)}, s32[512]{0:T(512)S(1)}, u32[]{:S(2)}, u32[]{:S(2)}) collective-permute-start(s32[512]{0:T(512)S(1)} %get-tuple-element.28), channel_id=1, source_target_pairs={{13,0},{14,1},{15,2},{0,3},{1,4},{2,5},{3,6},{4,7},{5,8},{6,9},{7,... | collective-permute-start | bytes 6152 | tf_op jit(solution)/shard_map/ppermute | solution.py:229
  35.1 29.7 %copy-start = (bf16[16384,128]{1,0:T(8,128)(2,1)S(1)}, bf16[16384,128]{1,0:T(8,128)(2,1)}, u32[]{:S(2)}) copy-start(bf16[16384,128]{1,0:T(8,128)(2,1)} %z_ref.1) | copy-start | bytes 12582916
  201.8 7.6 %collective-permute-start.5 = (bf16[512,128]{1,0:T(8,128)(2,1)S(1)}, bf16[512,128]{1,0:T(8,128)(2,1)S(1)}, u32[]{:S(2)}, u32[]{:S(2)}) collective-permute-start(bf16[512,128]{1,0:T(8,128)(2,1)S(1)} %get-tuple-element.11), channel_id=1, source_target_pairs={{15,0},{0,1},{1,2},{2,3},{3,4},{4,5},{5,6},{6,7},{7,8},{8,9},{9,10... | collective-permute-start | bytes 393224 | tf_op jit(solution)/shard_map/ppermute | solution.py:229
  202.2 8.8 %collective-permute-start.6 = (bf16[512,128]{1,0:T(8,128)(2,1)S(1)}, bf16[512,128]{1,0:T(8,128)(2,1)S(1)}, u32[]{:S(2)}, u32[]{:S(2)}) collective-permute-start(bf16[512,128]{1,0:T(8,128)(2,1)S(1)} %get-tuple-element.12), channel_id=1, source_target_pairs={{14,0},{15,1},{0,2},{1,3},{2,4},{3,5},{4,6},{5,7},{6,8},{7,9},{8,1... | collective-permute-start | bytes 393224 | tf_op jit(solution)/shard_map/ppermute | solution.py:229
  204.3 6.6 %collective-permute-start.7 = (bf16[512,128]{1,0:T(8,128)(2,1)S(1)}, bf16[512,128]{1,0:T(8,128)(2,1)S(1)}, u32[]{:S(2)}, u32[]{:S(2)}) collective-permute-start(bf16[512,128]{1,0:T(8,128)(2,1)S(1)} %get-tuple-element.13), channel_id=1, source_target_pairs={{13,0},{14,1},{15,2},{0,3},{1,4},{2,5},{3,6},{4,7},{5,8},{6,9},{7,... | collective-permute-start | bytes 393224 | tf_op jit(solution)/shard_map/ppermute | solution.py:229
  229.6 6.4 %collective-permute-start.8 = (bf16[256,128]{1,0:T(8,128)(2,1)S(1)}, bf16[256,128]{1,0:T(8,128)(2,1)S(1)}, u32[]{:S(2)}, u32[]{:S(2)}) collective-permute-start(bf16[256,128]{1,0:T(8,128)(2,1)S(1)} %gather_fusion.2), channel_id=1, source_target_pairs={{15,0},{0,1},{1,2},{2,3},{3,4},{4,5},{5,6},{6,7},{7,8},{8,9},{9,10... | collective-permute-start | bytes 196616 | tf_op jit(solution)/shard_map/ppermute | solution.py:229
  232.3 3.8 %collective-permute-start.9 = (bf16[256,128]{1,0:T(8,128)(2,1)S(1)}, bf16[256,128]{1,0:T(8,128)(2,1)S(1)}, u32[]{:S(2)}, u32[]{:S(2)}) collective-permute-start(bf16[256,128]{1,0:T(8,128)(2,1)S(1)} %gather_fusion.2), channel_id=1, source_target_pairs={{1,0},{2,1},{3,2},{4,3},{5,4},{6,5},{7,6},{8,7},{9,8},{10,9},{11,1... | collective-permute-start | bytes 196616 | tf_op jit(solution)/shard_map/ppermute | solution.py:229
  258.5 8.3 %collective-permute-start.10 = (bf16[512,128]{1,0:T(8,128)(2,1)S(1)}, bf16[512,128]{1,0:T(8,128)(2,1)S(1)}, u32[]{:S(2)}, u32[]{:S(2)}) collective-permute-start(bf16[512,128]{1,0:T(8,128)(2,1)S(1)} %get-tuple-element.8), channel_id=1, source_target_pairs={{1,0},{2,1},{3,2},{4,3},{5,4},{6,5},{7,6},{8,7},{9,8},{10,9},{11,1... | collective-permute-start | bytes 393224 | tf_op jit(solution)/shard_map/ppermute | solution.py:229
  263.0 6.2 %collective-permute-start.11 = (bf16[512,128]{1,0:T(8,128)(2,1)S(1)}, bf16[512,128]{1,0:T(8,128)(2,1)S(1)}, u32[]{:S(2)}, u32[]{:S(2)}) collective-permute-start(bf16[512,128]{1,0:T(8,128)(2,1)S(1)} %get-tuple-element.9), channel_id=1, source_target_pairs={{2,0},{3,1},{4,2},{5,3},{6,4},{7,5},{8,6},{9,7},{10,8},{11,9},{12,... | collective-permute-start | bytes 393224 | tf_op jit(solution)/shard_map/ppermute | solution.py:229
  263.0 7.6 %collective-permute-start.12 = (bf16[512,128]{1,0:T(8,128)(2,1)S(1)}, bf16[512,128]{1,0:T(8,128)(2,1)S(1)}, u32[]{:S(2)}, u32[]{:S(2)}) collective-permute-start(bf16[512,128]{1,0:T(8,128)(2,1)S(1)} %get-tuple-element.10), channel_id=1, source_target_pairs={{3,0},{4,1},{5,2},{6,3},{7,4},{8,5},{9,6},{10,7},{11,8},{12,9},{13... | collective-permute-start | bytes 393224 | tf_op jit(solution)/shard_map/ppermute | solution.py:229

commit v3 on v2

--- a/solution.py
+++ b/solution.py
@@ -25,33 +25,37 @@
     even, odd = rest[-2:]
     count = rows // CHUNK
 
-    def gather(chunk, target, degrees=range(degree)):
+    edges = degree * CHUNK
+    share = -(-edges // (degree + 3))
+
+    def gather(chunk, target, low, high):
         base = chunk * CHUNK
-        for k in degrees:
-            for j in range(CHUNK):
-                r = k * CHUNK + j
-                target[r : r + 1, :] = far_ref[idx_ref[base + (k * rows + j)]]
+        for r in range(low, min(high, edges)):
+            k, j = divmod(r, CHUNK)
+            target[r : r + 1, :] = far_ref[idx_ref[base + (k * rows + j)]]
 
     def compute(chunk, source, following, target):
         start = pl.multiple_of(chunk * CHUNK, CHUNK)
         z = z_ref[pl.ds(start, CHUNK), :]
         both = jnp.dot(z, own_ref[...], preferred_element_type=jnp.float32)
+        gather(following, target, 0, share)
         width = z.shape[1]
         own = 0.5 * (both[:, :width] + bias_ref[0:1, :])
         node = both[:, width:] + bias_ref[1:2, :]
         agg = None
         for k in range(degree):
-            gather(following, target, (k,))
             hidden = half_silu(source[k * CHUNK : (k + 1) * CHUNK, :] + own).astype(jnp.bfloat16)
-            msg = half_silu(
-                0.5 * jnp.dot(hidden, mid_ref[...], preferred_element_type=jnp.float32)
-            )
+            product = jnp.dot(hidden, mid_ref[...], preferred_element_type=jnp.float32)
+            gather(following, target, (k + 1) * share, (k + 2) * share)
+            msg = half_silu(0.5 * product)
             agg = msg if agg is None else agg + msg
         pre = node + jnp.dot(
             agg.astype(jnp.bfloat16), mix_ref[...], preferred_element_type=jnp.float32
         )
+        gather(following, target, (degree + 1) * share, (degree + 2) * share)
         inner = half_silu(0.5 * pre).astype(jnp.bfloat16)
         update = jnp.dot(inner, last_ref[...], preferred_element_type=jnp.float32)
+        gather(following, target, (degree + 2) * share, edges)
         if keep:
             update = (z.astype(jnp.float32) + update).astype(jnp.bfloat16)
         else:
@@ -59,7 +63,7 @@
             update = update.astype(jnp.bfloat16)
         out_ref[pl.ds(start, CHUNK), :] = update.astype(jnp.float32)
 
-    gather(0, even)
+    gather(0, even, 0, edges)
 
     def pair(p, carry):
         first = p * 2
@@ -70,17 +74,47 @@
     lax.fori_loop(0, count // 2, pair, 0)
 
 
+def far_kernel(states_ref, low_ref, mine_ref, high_ref, proj_ref, out_ref):
+    count, tile = states_ref.shape[0], 1024
+
+    def some(c, carry):
+        start = pl.multiple_of(c * tile, tile)
+        out_ref[pl.ds(start, tile), :] = 0.5 * jnp.dot(
+            states_ref[pl.ds(start, tile), :], proj_ref[...], preferred_element_type=jnp.float32
+        )
+        return carry
+
+    lax.fori_loop(0, count // tile, some, 0)
+    size = low_ref.shape[0]
+    for n, part in enumerate((low_ref, mine_ref, high_ref)):
+        out_ref[count + n * size : count + (n + 1) * size, :] = 0.5 * jnp.dot(
+            part[...], proj_ref[...], preferred_element_type=jnp.float32
+        )
+
+
+def far_table(states, halo, proj):
+    whole = pl.BlockSpec(memory_space=pltpu.VMEM)
+    rows = states.shape[0] + sum(part.shape[0] for part in halo)
+    return pl.pallas_call(
+        far_kernel,
+        in_specs=[whole] * 5,
+        out_specs=whole,
+        out_shape=jax.ShapeDtypeStruct((rows, states.shape[1]), jnp.float32),
+        compiler_params=pltpu.CompilerParams(vmem_limit_bytes=VMEM_LIMIT),
+    )(states, *halo, proj)
+
+
 def by_row(table):
     return lax.optimization_barrier(table).reshape(table.shape[0], 1, table.shape[1])
 
 
-def message_layer(states, table, neighbor_idx, edge_proj, node_proj, bias_pair, keep):
+def message_layer(states, halo, neighbor_idx, edge_proj, node_proj, bias_pair, keep):
     count_rows, width = states.shape
     degree = neighbor_idx.shape[0]
     rows = min(2048, count_rows)
     blocks = count_rows // rows
-    far = 0.5 * jnp.dot(table, edge_proj[1], preferred_element_type=jnp.float32)
-    far = by_row(far)
+    table = far_table(states, halo, edge_proj[1])
+    far = by_row(table)
     order = neighbor_idx.reshape(degree, blocks, rows).transpose(1, 0, 2).reshape(-1)
     own = jnp.concatenate([edge_proj[0], node_proj[0]], axis=1)
     whole = pl.BlockSpec(memory_space=pltpu.VMEM)
@@ -229,8 +263,8 @@
     return lax.ppermute(block, AXES, [((i - distance) % count, i) for i in range(count)])
 
 
-def extended(table, block):
-    return jnp.concatenate([table, from_behind(block, 1), block, from_behind(block, -1)], axis=0)
+def halo_of(block):
+    return from_behind(block, 1), block, from_behind(block, -1)
 
 
 def on_device(
@@ -248,7 +282,7 @@
     coarse_rows = local_rows // RATIO
     spill = local_rows // 32
     local_count = local_rows - (REACH - 1) * spill
-    neighbor_table = extended(features, features[send_rows])
+    fine_halo = halo_of(features[send_rows])
 
     num_parts = lax.axis_size(AXES)
     position = lax.axis_index(AXES)
@@ -278,16 +312,16 @@
     )[: coarse_rows * RATIO] % members
 
     (fine_out,) = message_layer(
-        features, neighbor_table, fine_nbrs, edge_weights[0], node_weights[0], biases[0], True
+        features, fine_halo, fine_nbrs, edge_weights[0], node_weights[0], biases[0], True
     )
     leaving_rows = fine_out[remote].astype(jnp.bfloat16)
     arrived_rows = jnp.concatenate(
         [from_behind(leaving_rows[(d - 1) * spill : d * spill], d) for d in range(1, REACH)], axis=0
     ).astype(jnp.float32)
     coarse_in = pool(by_row(fine_out), by_row(arrived_rows), grouped, coarse_rows)
-    coarse_table = extended(coarse_in, coarse_in[coarse_send])
+    coarse_halo = halo_of(coarse_in[coarse_send])
     coarse_float, coarse_update = message_layer(
-        coarse_in, coarse_table, coarse_nbrs, edge_weights[1], node_weights[1], biases[1], False
+        coarse_in, coarse_halo, coarse_nbrs, edge_weights[1], node_weights[1], biases[1], False
     )
     answers = coarse_update[jnp.concatenate(arrived_slots)]
     returned = jnp.concatenate(

time: 290 us -> 270 us (0.931)
  matrix products: 31.2 us -> 0.45 us
  Pallas kernels: 184 us -> 193 us
    dot_general x2 -> x0, matrix products: 30.8 us -> none  [message_layer(): far = 0.5 * jnp.dot(table, edge_proj[1], preferred_element_type=jnp.float32)]
    pallas_call x0 -> x2, Pallas kernels: none -> 7.76 us  [far_table(): pl.pallas_call(far_kernel, in_specs=[whole] * 5, out_specs=whole, out_sha...]
  transfers between devices with their start and end apart: 13 -> 13, of which waited for: 6 -> 7; matrix products, arithmetic and copies ran while one was open for 8% -> 8% of each run, Pallas kernels for 0% -> 0%
where the time goes in v3:
time: 270 us; the launch traced here: 269 us
  Pallas kernels  193 us (71%)
  starting transfers between devices  20.8 us (8%)
  local copies, waits for them, and re-layouts  20.3 us (8%)
  other arithmetic  18.7 us (7%)
  waiting for transfers between devices  14.7 us (5%)
    pallas_call x2, Pallas kernels, message_layer(): pl.pallas_call(functools.partial(layer_kernel, degree, rows, keep), grid=...  150 us
    ppermute x13, starting transfers between devices, from_behind(): lax.ppermute(block, AXES, [((i - distance) % count, i) for i in range(cou...  20.8 us
    pallas_call x1, Pallas kernels, spread(): pl.pallas_call(functools.partial(spread_kernel, rows, near, far), grid=(c...  18 us
    pallas_call x1, Pallas kernels, pool(): pl.pallas_call(functools.partial(pool_kernel, rows), grid=(coarse_rows //...  17.8 us
    ppermute x13, waiting for transfers between devices, from_behind(): lax.ppermute(block, AXES, [((i - distance) % count, i) for i in range(cou...  14.7 us
    sort x1, other arithmetic, on_device(): lax.sort(keys * members + jnp.arange(keys.shape[0], dtype=jnp.int32), is_...  8.68 us
    pallas_call x2, Pallas kernels, far_table(): pl.pallas_call(far_kernel, in_specs=[whole] * 5, out_specs=whole, out_sha...  7.76 us
    sort x1, other arithmetic, on_device(): lax.sort((reach_index * local_rows + place) * coarse_rows + slot_index, i...  6.28 us
  transfers between devices with their start and end apart: 13, of which 7 were waited for; matrix products, arithmetic and copies ran while one was open for 8% of the time, Pallas kernels for 0%

profile of v3, /device:TPU:0, one launch (start us, length us, event | category | flops | bytes accessed | tf_op | source)
XLA Modules:
  0.0 269.1 jit_solution(335288006592674062)
XLA Ops:
  0.6 0.7 compare_select_fusion.2
  1.4 3.8 %gather_fusion = bf16[512,128]{1,0:T(8,128)(2,1)S(1)} fusion(bf16[16384,128]{1,0:T(8,128)(2,1)} %z_ref.1, s32[1024]{0:T(1024)S(1)} %pad_clamp_fusion.3), kind=kCustom, calls=%fused_computation | custom fusion | bytes 264192 | tf_op jit(solution)/shard_map/gather | solution.py:285
  5.7 5.0 %collective-permute-start.1 = (bf16[512,128]{1,0:T(8,128)(2,1)S(1)}, bf16[512,128]{1,0:T(8,128)(2,1)S(1)}, u32[]{:S(2)}, u32[]{:S(2)}) collective-permute-start(bf16[512,128]{1,0:T(8,128)(2,1)S(1)} %gather_fusion), channel_id=1, source_target_pairs={{1,0},{2,1},{3,2},{4,3},{5,4},{6,5},{7,6},{8,7},{9,8},{10,9},{11,1... | collective-permute-start | bytes 393224 | tf_op jit(solution)/shard_map/ppermute | solution.py:263
  10.7 0.9 fusion.32
  12.3 1.0 broadcast_select_fusion
  13.2 6.3 %sort.14 = s32[16384]{0:T(1024)S(1)} sort(s32[16384]{0:T(1024)S(1)} %get-tuple-element.27), dimensions={0}, to_apply=%region_2.3 | sort | flops 229376 | bytes 131072 | tf_op jit(solution)/shard_map/sort | solution.py:297
  19.7 1.6 collective-permute-start.4
  21.3 0.9 slice_bitcast_fusion
  22.2 0.9 slice_bitcast_fusion.2
  24.4 1.2 reshape.201.idx_ref
  26.0 8.7 %sort.15 = s32[17920]{0:T(1024)S(1)} sort(s32[17920]{0:T(1024)S(1)} %fusion.6), dimensions={0}, to_apply=%region_3.4 | sort | flops 268800 | bytes 143360 | tf_op jit(solution)/shard_map/sort | solution.py:310
  34.7 2.2 copy-done
  36.9 7.2 %shard_map.104 = f32[17920,128]{1,0:T(8,128)} custom-call(bf16[16384,128]{1,0:T(8,128)(2,1)S(1)} %copy-done, bf16[512,128]{1,0:T(8,128)(2,1)S(1)} %collective-permute-done.low_ref, bf16[512,128]{1,0:T(8,128)(2,1)S(1)} %gather_fusion, bf16[512,128]{1,0:T(8,128)(2,1)S(1)} %collective-permute-done.1.high_ref, bf16[128,128]{1,0:T(8,128)(2,1)S(1)} %get-tuple-element.24.proj_ref), custom_call_target="tpu_custom_call" | custom-call | tf_op jit(solution)/shard_map/pallas_call | solution.py:98
  44.0 131.9 %shard_map.105.fine_ref = f32[16384,128]{1,0:T(8,128)} custom-call(s32[98304]{0:T(1024)S(1)} %reshape.201.idx_ref, bf16[16384,128]{1,0:T(8,128)(2,1)S(1)} %copy-done, f32[17920,1,128]{2,1,0:T(1,128)} %bitcast.55, bf16[128,256]{1,0:T(8,128)(2,1)S(1)} %get-tuple-element.34.own_ref, bf16[128,128]{1,0:T(8,128)(2,1)S(1)} %get-tuple-element.22.mid_ref, ...), custom_call_target="tpu_custom_call" | custom-call | flops 3221225472 | bytes 21757952 | tf_op jit(solution)/shard_map/pallas_call | solution.py:123
  176.0 6.0 %gather_fusion.1 = bf16[1536,128]{1,0:T(8,128)(2,1)S(1)} fusion(f32[16384,128]{1,0:T(8,128)} %shard_map.105.fine_ref, s32[2048]{0:T(1024)S(1)} %pad_clamp_fusion.1), kind=kCustom, calls=%fused_computation.1 | custom fusion | bytes 792576 | tf_op jit(solution)/shard_map/gather | solution.py:317
  182.0 0.9 collective-permute-start.5
  182.9 1.4 collective-permute-start.6
  184.3 2.4 collective-permute-start.7
  186.7 2.5 collective-permute-done.5
  189.2 2.4 collective-permute-done.6
  191.7 17.8 %shard_map.106.states_ref.z_ref = bf16[2048,128]{1,0:T(8,128)(2,1)S(1)} custom-call(s32[16384]{0:T(1024)S(1)} %add_select_fusion.idx_ref, f32[16384,1,128]{2,1,0:T(1,128)} %bitcast.54, f32[1536,1,128]{2,1,0:T(1,128)S(1)} %bitcast.51), custom_call_target="tpu_custom_call" | custom-call | tf_op jit(solution)/shard_map/pallas_call | solution.py:180
  209.5 0.9 gather_fusion.2
  210.3 2.7 collective-permute-start.8
  213.0 1.8 collective-permute-start.9
  214.8 1.9 collective-permute-done.8.low_ref
  217.4 17.7 %shard_map.108 = (f32[2048,128]{1,0:T(8,128)S(1)}, bf16[2048,128]{1,0:T(8,128)(2,1)}) custom-call(s32[12288]{0:T(1024)S(1)} %reshape_transpose_reshape.3.idx_ref, bf16[2048,128]{1,0:T(8,128)(2,1)S(1)} %shard_map.106.states_ref.z_ref, f32[2816,1,128]{2,1,0:T(1,128)S(1)} %bitcast.52, bf16[128,256]{1,0:T(8,128)(2,1)S(1)} %get-tuple-element.35.own_ref, ...), custom_call_target="tpu_custom_call" | custom-call | flops 402653184 | bytes 3014656 | tf_op jit(solution)/shard_map/pallas_call | solution.py:123
  235.1 3.8 %gather_fusion.3 = bf16[1536,128]{1,0:T(8,128)(2,1)S(1)} fusion(bf16[2048,128]{1,0:T(8,128)(2,1)} %get-tuple-element.3, s32[2048]{0:T(1024)S(1)} %pad_clamp_fusion), kind=kCustom, calls=%fused_computation.3 | custom fusion | bytes 792576 | tf_op jit(solution)/shard_map/gather | solution.py:326
  238.9 4.5 %collective-permute-start.10 = (bf16[512,128]{1,0:T(8,128)(2,1)S(1)}, bf16[512,128]{1,0:T(8,128)(2,1)S(1)}, u32[]{:S(2)}, u32[]{:S(2)}) collective-permute-start(bf16[512,128]{1,0:T(8,128)(2,1)S(1)} %get-tuple-element.8), channel_id=1, source_target_pairs={{1,0},{2,1},{3,2},{4,3},{5,4},{6,5},{7,6},{8,7},{9,8},{10,9},{11,1... | collective-permute-start | bytes 393224 | tf_op jit(solution)/shard_map/ppermute | solution.py:263
  243.3 3.8 %collective-permute-done.10 = bf16[512,128]{1,0:T(8,128)(2,1)S(1)} collective-permute-done((bf16[512,128]{1,0:T(8,128)(2,1)S(1)}, bf16[512,128]{1,0:T(8,128)(2,1)S(1)}, u32[]{:S(2)}, u32[]{:S(2)}) %collective-permute-start.10) | collective-permute-done | bytes 131104 | tf_op jit(solution)/shard_map/ppermute | solution.py:263
  247.1 2.4 collective-permute-done.11
  249.5 1.4 collective-permute-done.12
  251.0 18.0 %shard_map.109 = bf16[16384,128]{1,0:T(8,128)(2,1)} custom-call(s32[16384]{0:T(1024)S(1)} %get-tuple-element.28.idx_ref, f32[16384,128]{1,0:T(8,128)} %shard_map.105.fine_ref, f32[2048,1,128]{2,1,0:T(1,128)S(1)} %bitcast.53, f32[1536,1,128]{2,1,0:T(1,128)S(1)} %bitcast.50), custom_call_target="tpu_custom_call" | custom-call | tf_op jit(solution)/shard_map/pallas_call | solution.py:227
  (39 shorter events, 3.9 us)
Async XLA Ops:
  0.6 25.0 %copy-start.1 = (s32[6,2048]{1,0:T(8,128)S(1)}, s32[6,2048]{1,0:T(8,128)}, u32[]{:S(2)}) copy-start(s32[6,2048]{1,0:T(8,128)} %param.14) | copy-start | bytes 147460
  5.2 29.5 %collective-permute-start = (bf16[512,128]{1,0:T(8,128)(2,1)S(1)}, bf16[512,128]{1,0:T(8,128)(2,1)S(1)}, u32[]{:S(2)}, u32[]{:S(2)}) collective-permute-start(bf16[512,128]{1,0:T(8,128)(2,1)S(1)} %gather_fusion), channel_id=1, source_target_pairs={{15,0},{0,1},{1,2},{2,3},{3,4},{4,5},{5,6},{6,7},{7,8},{8,9},{9,10... | collective-permute-start | bytes 393224 | tf_op jit(solution)/shard_map/ppermute | solution.py:263
  5.7 29.0 %collective-permute-start.1 = (bf16[512,128]{1,0:T(8,128)(2,1)S(1)}, bf16[512,128]{1,0:T(8,128)(2,1)S(1)}, u32[]{:S(2)}, u32[]{:S(2)}) collective-permute-start(bf16[512,128]{1,0:T(8,128)(2,1)S(1)} %gather_fusion), channel_id=1, source_target_pairs={{1,0},{2,1},{3,2},{4,3},{5,4},{6,5},{7,6},{8,7},{9,8},{10,9},{11,1... | collective-permute-start | bytes 393224 | tf_op jit(solution)/shard_map/ppermute | solution.py:263
  19.6 6.1 %collective-permute-start.2 = (s32[512]{0:T(512)S(1)}, s32[512]{0:T(512)S(1)}, u32[]{:S(2)}, u32[]{:S(2)}) collective-permute-start(s32[512]{0:T(512)S(1)} %get-tuple-element.29), channel_id=1, source_target_pairs={{15,0},{0,1},{1,2},{2,3},{3,4},{4,5},{5,6},{6,7},{7,8},{8,9},{9,10... | collective-permute-start | bytes 6152 | tf_op jit(solution)/shard_map/ppermute | solution.py:263
  19.6 6.3 %collective-permute-start.3 = (s32[512]{0:T(512)S(1)}, s32[512]{0:T(512)S(1)}, u32[]{:S(2)}, u32[]{:S(2)}) collective-permute-start(s32[512]{0:T(512)S(1)} %get-tuple-element.31), channel_id=1, source_target_pairs={{14,0},{15,1},{0,2},{1,3},{2,4},{3,5},{4,6},{5,7},{6,8},{7,9},{8,1... | collective-permute-start | bytes 6152 | tf_op jit(solution)/shard_map/ppermute | solution.py:263
  19.7 6.3 %collective-permute-start.4 = (s32[512]{0:T(512)S(1)}, s32[512]{0:T(512)S(1)}, u32[]{:S(2)}, u32[]{:S(2)}) collective-permute-start(s32[512]{0:T(512)S(1)} %get-tuple-element.30), channel_id=1, source_target_pairs={{13,0},{14,1},{15,2},{0,3},{1,4},{2,5},{3,6},{4,7},{5,8},{6,9},{7,... | collective-permute-start | bytes 6152 | tf_op jit(solution)/shard_map/ppermute | solution.py:263
  34.7 2.2 copy-start
  182.0 7.1 %collective-permute-start.5 = (bf16[512,128]{1,0:T(8,128)(2,1)S(1)}, bf16[512,128]{1,0:T(8,128)(2,1)S(1)}, u32[]{:S(2)}, u32[]{:S(2)}) collective-permute-start(bf16[512,128]{1,0:T(8,128)(2,1)S(1)} %get-tuple-element.11), channel_id=1, source_target_pairs={{15,0},{0,1},{1,2},{2,3},{3,4},{4,5},{5,6},{6,7},{7,8},{8,9},{9,10... | collective-permute-start | bytes 393224 | tf_op jit(solution)/shard_map/ppermute | solution.py:263
  182.9 8.7 %collective-permute-start.6 = (bf16[512,128]{1,0:T(8,128)(2,1)S(1)}, bf16[512,128]{1,0:T(8,128)(2,1)S(1)}, u32[]{:S(2)}, u32[]{:S(2)}) collective-permute-start(bf16[512,128]{1,0:T(8,128)(2,1)S(1)} %get-tuple-element.12), channel_id=1, source_target_pairs={{14,0},{15,1},{0,2},{1,3},{2,4},{3,5},{4,6},{5,7},{6,8},{7,9},{8,1... | collective-permute-start | bytes 393224 | tf_op jit(solution)/shard_map/ppermute | solution.py:263
  184.3 7.3 %collective-permute-start.7 = (bf16[512,128]{1,0:T(8,128)(2,1)S(1)}, bf16[512,128]{1,0:T(8,128)(2,1)S(1)}, u32[]{:S(2)}, u32[]{:S(2)}) collective-permute-start(bf16[512,128]{1,0:T(8,128)(2,1)S(1)} %get-tuple-element.13), channel_id=1, source_target_pairs={{13,0},{14,1},{15,2},{0,3},{1,4},{2,5},{3,6},{4,7},{5,8},{6,9},{7,... | collective-permute-start | bytes 393224 | tf_op jit(solution)/shard_map/ppermute | solution.py:263
  210.3 6.4 %collective-permute-start.8 = (bf16[256,128]{1,0:T(8,128)(2,1)S(1)}, bf16[256,128]{1,0:T(8,128)(2,1)S(1)}, u32[]{:S(2)}, u32[]{:S(2)}) collective-permute-start(bf16[256,128]{1,0:T(8,128)(2,1)S(1)} %gather_fusion.2), channel_id=1, source_target_pairs={{15,0},{0,1},{1,2},{2,3},{3,4},{4,5},{5,6},{6,7},{7,8},{8,9},{9,10... | collective-permute-start | bytes 196616 | tf_op jit(solution)/shard_map/ppermute | solution.py:263
  213.0 3.8 %collective-permute-start.9 = (bf16[256,128]{1,0:T(8,128)(2,1)S(1)}, bf16[256,128]{1,0:T(8,128)(2,1)S(1)}, u32[]{:S(2)}, u32[]{:S(2)}) collective-permute-start(bf16[256,128]{1,0:T(8,128)(2,1)S(1)} %gather_fusion.2), channel_id=1, source_target_pairs={{1,0},{2,1},{3,2},{4,3},{5,4},{6,5},{7,6},{8,7},{9,8},{10,9},{11,1... | collective-permute-start | bytes 196616 | tf_op jit(solution)/shard_map/ppermute | solution.py:263
  238.9 8.3 %collective-permute-start.10 = (bf16[512,128]{1,0:T(8,128)(2,1)S(1)}, bf16[512,128]{1,0:T(8,128)(2,1)S(1)}, u32[]{:S(2)}, u32[]{:S(2)}) collective-permute-start(bf16[512,128]{1,0:T(8,128)(2,1)S(1)} %get-tuple-element.8), channel_id=1, source_target_pairs={{1,0},{2,1},{3,2},{4,3},{5,4},{6,5},{7,6},{8,7},{9,8},{10,9},{11,1... | collective-permute-start | bytes 393224 | tf_op jit(solution)/shard_map/ppermute | solution.py:263
  243.3 6.2 %collective-permute-start.11 = (bf16[512,128]{1,0:T(8,128)(2,1)S(1)}, bf16[512,128]{1,0:T(8,128)(2,1)S(1)}, u32[]{:S(2)}, u32[]{:S(2)}) collective-permute-start(bf16[512,128]{1,0:T(8,128)(2,1)S(1)} %get-tuple-element.9), channel_id=1, source_target_pairs={{2,0},{3,1},{4,2},{5,3},{6,4},{7,5},{8,6},{9,7},{10,8},{11,9},{12,... | collective-permute-start | bytes 393224 | tf_op jit(solution)/shard_map/ppermute | solution.py:263
  243.3 7.6 %collective-permute-start.12 = (bf16[512,128]{1,0:T(8,128)(2,1)S(1)}, bf16[512,128]{1,0:T(8,128)(2,1)S(1)}, u32[]{:S(2)}, u32[]{:S(2)}) collective-permute-start(bf16[512,128]{1,0:T(8,128)(2,1)S(1)} %get-tuple-element.10), channel_id=1, source_target_pairs={{3,0},{4,1},{5,2},{6,3},{7,4},{8,5},{9,6},{10,7},{11,8},{12,9},{13... | collective-permute-start | bytes 393224 | tf_op jit(solution)/shard_map/ppermute | solution.py:263
